TPU v7x, 32 devices: a whole 2x2x4 slice. The times are simulated.
32 devices in a mesh: ka: 4 (over x, core), fit: 8 (over z, y).
Axes of the slice: x: 2, y: 2, z: 4, core: 2. Of those that a mesh axis runs over, the one named last changes fastest.
Arguments:
- integrals: bfloat16 [3, 4, 8, 48, 64, 128], P(None, 'ka', 'fit'), may hold values from -0.3125 to 0.3125
- block_lists: int32 [3, 4, 8, 2, 48], P(None, 'ka', 'fit'), may hold values from 0 to 15, as said below
- coeff: bfloat16 [4, 2, 1024, 256], P('ka', None, 'fit'), may hold values from -6 to 6
- match: int32 [3, 4], replicated, may hold values from 0 to 3, each once within a row
- ex_blocks: int32 [4, 2, 64], P('ka'), may hold values from 0 to 15, as said below
Outputs:
- exchange: float32 [4, 4096, 128], P('ka', 'fit')
Inputs may be any that keep to these rules, and one draw needn't show every extreme that they name: `block_lists`: each integral matrix lists 48 distinct blocks; each entry is a block index below 16, row first then column. `ex_blocks`: each k-point lists 64 distinct blocks, none on the diagonal (row block differs from column block).
All inputs are finite; a program needn't handle non-finite values.
Results may differ from a plain program's by a relative error of at most 0.0036.
Values may be sent and summed in bfloat16 or wider, within the bound.
No kernel may reach another device: no remote copies, remote signals or barrier semaphores. Data moves between devices by JAX's collectives and lax.ppermute only.
A program may use at most 128 MiB of HBM per device.

v0:
```python
import functools

import jax
import jax.numpy as jnp
from jax import lax
from jax.experimental import pallas as pl
from jax.experimental.pallas import tpu as pltpu
from jax.sharding import PartitionSpec as P

AXES = ("ka", "fit")
TILE = 16


def bits_of(size):
    return [1 << b for b in range(size.bit_length() - 1)]


def near_dims(nka, nfit):
    low, second = bits_of(nfit)[:2]
    return (nka // 2, 0), (0, low), (0, second)


def gather_orders(nka, nfit):
    x, y, w = near_dims(nka, nfit)
    return ((x, y, w), (y, w, x)), ((w, x, y), (w, x, y))


def swap_by(arr, nka, nfit, by_core):
    perm = []
    for k in range(nka):
        dka, dfit = by_core[k & 1]
        for f in range(nfit):
            perm.append((k * nfit + f, (k ^ dka) * nfit + (f ^ dfit)))
    return lax.ppermute(arr, AXES, perm)


def far_offsets(nfit):
    offsets = [0]
    for bit in bits_of(nfit)[2:]:
        offsets = offsets + [o ^ bit for o in offsets]
    return offsets


def split_row(rows):
    return (2 * rows // 3 + TILE // 2) // TILE * TILE


def gather_shards(shard, nka, nfit):
    stack = shard.reshape(-1, shard.shape[-1])
    for bit in bits_of(nfit)[2:]:
        stack = jnp.concatenate([stack, swap_by(stack, nka, nfit, [(0, bit)] * 2)], axis=0)
    cut = split_row(stack.shape[0])
    parts = [stack[:cut], stack[cut:]]
    orders = gather_orders(nka, nfit)
    for step in range(3):
        fresh = [
            swap_by(part, nka, nfit, [order[core][step] for core in range(2)])
            for part, order in zip(parts, orders)
        ]
        if step < 2:
            parts = [jnp.concatenate(pair, axis=0) for pair in zip(parts, fresh)]
    held = [arr for pair in zip(parts, fresh) for arr in pair]
    return held + [swap_by(arr, nka, nfit, [(1, 0)] * 2) for arr in held]


def exchange_units(owner_of, unit, edge, x_ref, turned_ref, ex_ref, out_ref):
    count, rows, _ = out_ref.shape
    for slot in range(count):
        for step in range(rows // unit):
            row = owner_of(slot) * rows + step * unit
            e = row // edge
            lb, rb = ex_ref[0, 0, e], ex_ref[0, 1, e]
            lo = pl.multiple_of(lax.rem(row, edge), unit)
            out_ref[slot, step * unit : (step + 1) * unit, :] = jnp.dot(
                x_ref[lb, pl.ds(lo, unit), :],
                turned_ref[rb],
                preferred_element_type=jnp.float32,
            ).astype(out_ref.dtype)


def scatter_owner(keep, nfit):
    low, second = bits_of(nfit)[:2]
    offs = far_offsets(nfit)
    core, fit = lax.rem(lax.axis_index("ka"), 2), lax.axis_index("fit")
    first = jnp.where(core == 0, low, second)
    other = low + second - first

    def owner(slot):
        off = offs[slot % len(offs)]
        owner = lax.bitwise_xor(fit, off)
        if slot >= len(offs):
            owner = lax.bitwise_xor(owner, other)
        return owner if keep else lax.bitwise_xor(owner, first)

    return owner


def half_kernel(
    nka, nfit, nq, nblk, edge, occ, nbl, rows, match_hbm, lists_hbm, ex_hbm, lmat_ref, *refs
):
    held = refs[:8]
    out_ref, x_ref, turned_ref = refs[8:11]
    match_ref, lists_ref, ex_ref, l_ref, ops_ref, sums_ref, sems, small = refs[11:]
    ka, fit = lax.axis_index("ka"), lax.axis_index("fit")
    core = lax.rem(ka, 2)
    sub = min(rows, edge)
    loads = [
        pltpu.make_async_copy(src, dst, small.at[i])
        for i, (src, dst) in enumerate(
            [(match_hbm, match_ref), (lists_hbm, lists_ref), (ex_hbm, ex_ref)]
        )
    ]
    copies = [
        pltpu.make_async_copy(lmat_ref.at[qq, 0, 0], l_ref.at[qq], sems.at[qq]) for qq in range(nq)
    ]
    for copy in loads + copies:
        copy.start()
    for copy in loads:
        copy.wait()

    far = far_offsets(nfit)
    orders = gather_orders(nka, nfit)
    total = len(far) * 2 * rows
    cut = split_row(total)
    spans = [(0, cut), (cut, total)]

    def place(ref, base, span, owner):
        lo, hi = span
        row = lo
        while row < hi:
            piece, rest = divmod(row, 2 * rows)
            part, inner = divmod(rest, rows)
            size = min(hi - row, sub - inner % sub)
            start = lax.bitwise_xor(owner, far[piece]) * rows + inner
            dst = (start // edge) * (2 * edge) + lax.rem(start, edge)
            dst = pl.multiple_of(dst, TILE)
            low = pl.multiple_of(dst + edge, TILE)
            value = ref[base + row - lo : base + row - lo + size, :]
            if part == 0:
                ops_ref[pl.ds(dst, size), :occ] = value
                ops_ref[pl.ds(low, size), occ:] = value
            else:
                ops_ref[pl.ds(dst, size), occ:] = value
                ops_ref[pl.ds(low, size), :occ] = -value
            row += size

    for qq in range(nq):
        want = match_ref[qq, ka]
        for whose in range(2):
            origin = lax.bitwise_xor(ka, whose)
            origin_core = lax.bitwise_xor(core, whose)
            for part in range(2):
                pair = orders[part]
                dims = [
                    [jnp.where(origin_core == 0, pair[0][s][i], pair[1][s][i]) for i in range(2)]
                    for s in range(3)
                ]
                length = spans[part][1] - spans[part][0]
                for slot in range(8):
                    owner_ka, owner_fit = origin, fit
                    for s in range(3):
                        if slot >> s & 1:
                            owner_ka = lax.bitwise_xor(owner_ka, dims[s][0])
                            owner_fit = lax.bitwise_xor(owner_fit, dims[s][1])
                    ref = held[whose * 4 + part * 2 + slot // 4]

                    @pl.when(want == owner_ka)
                    def _():
                        place(ref, slot % 4 * length, spans[part], owner_fit)

        sums_ref[...] = jnp.zeros_like(sums_ref)
        copies[qq].wait()

        def one_block(n, c):
            rb = pl.multiple_of(lists_ref[qq, 0, 0, 0, n] * edge, edge)
            cb = pl.multiple_of(lists_ref[qq, 0, 0, 1, n] * (2 * edge), 2 * edge)
            sums_ref[pl.ds(rb, edge), :] += jnp.dot(
                l_ref[qq, n],
                ops_ref[pl.ds(cb, 2 * edge), :],
                preferred_element_type=jnp.float32,
            )
            return c

        lax.fori_loop(0, nblk, one_block, 0, unroll=16)

        def one_row(rb, c):
            x = sums_ref[pl.ds(pl.multiple_of(rb * edge, edge), edge), :].astype(jnp.bfloat16)
            x_ref[rb, :, qq * 2 * occ : (qq + 1) * 2 * occ] = x
            low = jnp.concatenate([-x[:, occ:], x[:, :occ]], axis=1)
            turned_ref[rb, qq * 2 * occ : (qq + 1) * 2 * occ, :] = jnp.concatenate([x, low], axis=0).T
            return c

        lax.fori_loop(0, nbl, one_row, 0, unroll=4)

    unit = min(edge, out_ref.shape[1])
    exchange_units(scatter_owner(False, nfit), unit, edge, x_ref, turned_ref, ex_ref, out_ref)


def rest_kernel(nfit, edge, ex_hbm, x_ref, turned_ref, out_ref, ex_ref, sem):
    copy = pltpu.make_async_copy(ex_hbm, ex_ref, sem)
    copy.start()
    copy.wait()
    unit = min(edge, out_ref.shape[1])
    exchange_units(scatter_owner(True, nfit), unit, edge, x_ref, turned_ref, ex_ref, out_ref)


def on_device(nka, nfit, integrals, block_lists, coeff, match, ex_blocks):
    nq, _, _, nblk, edge, _ = integrals.shape
    rows, occ = coeff.shape[2:]
    nexch = ex_blocks.shape[2]
    nbl = nfit * rows // edge
    held = gather_shards(coeff, nka, nfit)
    vmem = pl.BlockSpec(memory_space=pltpu.VMEM)
    hbm = pl.BlockSpec(memory_space=pltpu.HBM)
    count, chunk = nfit // 2, nexch * edge // nfit
    params = pltpu.CompilerParams(vmem_limit_bytes=28 * 1024 * 1024)
    bf16, f32, i32 = jnp.bfloat16, jnp.float32, jnp.int32
    out, xmat, turned = pl.pallas_call(
        functools.partial(half_kernel, nka, nfit, nq, nblk, edge, occ, nbl, rows),
        out_shape=[
            jax.ShapeDtypeStruct((count, chunk, 2 * edge), bf16),
            jax.ShapeDtypeStruct((nbl, edge, nq * 2 * occ), bf16),
            jax.ShapeDtypeStruct((nbl, nq * 2 * occ, 2 * edge), bf16),
        ],
        in_specs=[hbm] * 4 + [vmem] * len(held),
        out_specs=[vmem] * 3,
        scratch_shapes=[
            pltpu.SMEM(match.shape, i32),
            pltpu.SMEM(block_lists.shape, i32),
            pltpu.SMEM(ex_blocks.shape, i32),
            pltpu.VMEM((nq, nblk, edge, 2 * edge), bf16),
            pltpu.VMEM((nbl * 2 * edge, 2 * occ), bf16),
            pltpu.VMEM((nbl * edge, 2 * occ), f32),
            pltpu.SemaphoreType.DMA((nq,)),
            pltpu.SemaphoreType.DMA((3,)),
        ],
        compiler_params=params,
    )(match, block_lists, ex_blocks, integrals, *held)
    own = pl.pallas_call(
        functools.partial(rest_kernel, nfit, edge),
        out_shape=jax.ShapeDtypeStruct((count, chunk, 2 * edge), f32),
        in_specs=[hbm, vmem, vmem],
        out_specs=vmem,
        scratch_shapes=[pltpu.SMEM(ex_blocks.shape, i32), pltpu.SemaphoreType.DMA],
        compiler_params=params,
        cost_estimate=pl.CostEstimate(
            flops=nexch * edge * edge * 2 * nq * 2 * occ, bytes_accessed=1 << 23, transcendentals=0
        ),
    )(ex_blocks, xmat, turned)

    low, second = [(0, bit) for bit in bits_of(nfit)[:2]]
    total = own + swap_by(out, nka, nfit, [low, second]).astype(f32)
    steps = [[second, low]] + [[(0, bit)] * 2 for bit in bits_of(nfit)[:1:-1]]
    for by_core in steps:
        n = total.shape[0] // 2
        came = swap_by(total[n:].astype(bf16), nka, nfit, by_core)
        total = total[:n] + came.astype(f32)
    factor = -((nq * nfit * occ) ** (-0.5))
    return total * factor


def solution(mesh):
    nka, nfit = mesh.shape["ka"], mesh.shape["fit"]
    return jax.shard_map(
        functools.partial(on_device, nka, nfit),
        mesh=mesh,
        in_specs=(
            P(None, "ka", "fit", None, None, None),
            P(None, "ka", "fit", None, None),
            P("ka", None, "fit", None),
            P(),
            P("ka", None, None),
        ),
        out_specs=P("ka", "fit", None),
        check_vma=False,
    )
```

profile of v0, /device:TPU:0, one launch (start us, length us, event | category | flops | bytes accessed | tf_op | source)
XLA Modules:
  0.0 86.0 jit_solution(16136768198056589252)
XLA Ops:
  0.0 4.0 %collective-permute-start = (bf16[256,256]{1,0:T(8,128)(2,1)}, bf16[256,256]{1,0:T(8,128)(2,1)S(1)}, u32[]{:S(2)}, u32[]{:S(2)}) collective-permute-start(bf16[256,256]{1,0:T(8,128)(2,1)} %bitcast.1), channel_id=1, source_target_pairs={{0,4},{1,5},{2,6},{3,7},{4,0},{5,1},{6,2},{7,3},{8,12},{9,13},{10,... | collective-permute-start | bytes 393224 | tf_op jit(solution)/shard_map/ppermute | solution.py:34
  4.0 6.5 %collective-permute-done = bf16[256,256]{1,0:T(8,128)(2,1)S(1)} collective-permute-done((bf16[256,256]{1,0:T(8,128)(2,1)}, bf16[256,256]{1,0:T(8,128)(2,1)S(1)}, u32[]{:S(2)}, u32[]{:S(2)}) %collective-permute-start) | collective-permute-done | bytes 131104 | tf_op jit(solution)/shard_map/ppermute | solution.py:34
  10.6 0.9 %pad_maximum_fusion.4 = bf16[336,256]{1,0:T(8,128)(2,1)S(1)} fusion(bf16[256,256]{1,0:T(8,128)(2,1)S(1)} %collective-permute-done, bf16[256,256]{1,0:T(8,128)(2,1)} %bitcast.2), kind=kLoop, calls=%fused_computation.10 | loop fusion | flops 344064 | bytes 434176 | tf_op jit(solution)/shard_map/concatenate | solution.py:51
  11.5 1.6 %collective-permute-start.1 = (bf16[336,256]{1,0:T(8,128)(2,1)S(1)}, bf16[336,256]{1,0:T(8,128)(2,1)S(1)}, u32[]{:S(2)}, u32[]{:S(2)}) collective-permute-start(bf16[336,256]{1,0:T(8,128)(2,1)S(1)} %pad_maximum_fusion.4), channel_id=1, source_target_pairs={{0,16},{1,17},{2,18},{3,19},{4,20},{5,21},{6,22},{7,23},{8,9},{9,8... | collective-permute-start | bytes 516104 | tf_op jit(solution)/shard_map/ppermute | solution.py:34
  13.1 3.9 %collective-permute-done.1 = bf16[336,256]{1,0:T(8,128)(2,1)S(1)} collective-permute-done((bf16[336,256]{1,0:T(8,128)(2,1)S(1)}, bf16[336,256]{1,0:T(8,128)(2,1)S(1)}, u32[]{:S(2)}, u32[]{:S(2)}) %collective-permute-start.1) | collective-permute-done | bytes 172064 | tf_op jit(solution)/shard_map/ppermute | solution.py:34
  17.0 0.0 copy-start
  17.0 0.0 copy-start.1
  17.0 0.0 copy-start.2
  17.0 0.0 copy-start.3
  17.0 1.6 %collective-permute-start.2 = (bf16[672,256]{1,0:T(8,128)(2,1)S(1)}, bf16[672,256]{1,0:T(8,128)(2,1)S(1)}, u32[]{:S(2)}, u32[]{:S(2)}) collective-permute-start(bf16[672,256]{1,0:T(8,128)(2,1)S(1)} %pad_maximum_fusion.2), channel_id=1, source_target_pairs={{0,1},{1,0},{2,3},{3,2},{4,5},{5,4},{6,7},{7,6},{8,10},{9,11},{10,... | collective-permute-start | bytes 1032200 | tf_op jit(solution)/shard_map/ppermute | solution.py:34
  18.7 5.7 %collective-permute-done.2 = bf16[672,256]{1,0:T(8,128)(2,1)S(1)} collective-permute-done((bf16[672,256]{1,0:T(8,128)(2,1)S(1)}, bf16[672,256]{1,0:T(8,128)(2,1)S(1)}, u32[]{:S(2)}, u32[]{:S(2)}) %collective-permute-start.2) | collective-permute-done | bytes 344096 | tf_op jit(solution)/shard_map/ppermute | solution.py:34
  24.4 0.9 %collective-permute-start.3 = (bf16[1344,256]{1,0:T(8,128)(2,1)S(1)}, bf16[1344,256]{1,0:T(8,128)(2,1)S(1)}, u32[]{:S(2)}, u32[]{:S(2)}) collective-permute-start(bf16[1344,256]{1,0:T(8,128)(2,1)S(1)} %pad_maximum_fusion.refs_0_), channel_id=1, source_target_pairs={{0,2},{1,3},{2,0},{3,1},{4,6},{5,7},{6,4},{7,5},{8,24},{9,25},{10,... | collective-permute-start | bytes 2064392 | tf_op jit(solution)/shard_map/ppermute | solution.py:34
  25.3 1.2 %collective-permute-start.4 = (bf16[176,256]{1,0:T(8,128)(2,1)S(1)}, bf16[176,256]{1,0:T(8,128)(2,1)S(1)}, u32[]{:S(2)}, u32[]{:S(2)}) collective-permute-start(bf16[176,256]{1,0:T(8,128)(2,1)S(1)} %slice.26), channel_id=1, source_target_pairs={{0,2},{1,3},{2,0},{3,1},{4,6},{5,7},{6,4},{7,5},{8,10},{9,11},{10,... | collective-permute-start | bytes 270344 | tf_op jit(solution)/shard_map/ppermute | solution.py:34
  26.5 9.9 %collective-permute-done.4 = bf16[176,256]{1,0:T(8,128)(2,1)S(1)} collective-permute-done((bf16[176,256]{1,0:T(8,128)(2,1)S(1)}, bf16[176,256]{1,0:T(8,128)(2,1)S(1)}, u32[]{:S(2)}, u32[]{:S(2)}) %collective-permute-start.4) | collective-permute-done | bytes 90144 | tf_op jit(solution)/shard_map/ppermute | solution.py:34
  36.4 1.6 %collective-permute-start.5 = (bf16[352,256]{1,0:T(8,128)(2,1)S(1)}, bf16[352,256]{1,0:T(8,128)(2,1)S(1)}, u32[]{:S(2)}, u32[]{:S(2)}) collective-permute-start(bf16[352,256]{1,0:T(8,128)(2,1)S(1)} %pad_maximum_fusion.3), channel_id=1, source_target_pairs={{0,16},{1,17},{2,18},{3,19},{4,20},{5,21},{6,22},{7,23},{8,24},{9,... | collective-permute-start | bytes 540680 | tf_op jit(solution)/shard_map/ppermute | solution.py:34
  38.0 4.0 %collective-permute-done.5 = bf16[352,256]{1,0:T(8,128)(2,1)S(1)} collective-permute-done((bf16[352,256]{1,0:T(8,128)(2,1)S(1)}, bf16[352,256]{1,0:T(8,128)(2,1)S(1)}, u32[]{:S(2)}, u32[]{:S(2)}) %collective-permute-start.5) | collective-permute-done | bytes 180256 | tf_op jit(solution)/shard_map/ppermute | solution.py:34
  42.0 1.6 %collective-permute-start.6 = (bf16[704,256]{1,0:T(8,128)(2,1)S(1)}, bf16[704,256]{1,0:T(8,128)(2,1)S(1)}, u32[]{:S(2)}, u32[]{:S(2)}) collective-permute-start(bf16[704,256]{1,0:T(8,128)(2,1)S(1)} %pad_maximum_fusion.1.refs_2_), channel_id=1, source_target_pairs={{0,1},{1,0},{2,3},{3,2},{4,5},{5,4},{6,7},{7,6},{8,9},{9,8},{10,11... | collective-permute-start | bytes 1081352 | tf_op jit(solution)/shard_map/ppermute | solution.py:34
  43.6 0.0 collective-permute-start.7
  43.6 0.0 collective-permute-done.3.refs_1_
  43.6 0.5 collective-permute-start.8
  44.1 0.0 collective-permute-start.9
  44.1 5.3 %collective-permute-done.6.refs_3_ = bf16[704,256]{1,0:T(8,128)(2,1)S(1)} collective-permute-done((bf16[704,256]{1,0:T(8,128)(2,1)S(1)}, bf16[704,256]{1,0:T(8,128)(2,1)S(1)}, u32[]{:S(2)}, u32[]{:S(2)}) %collective-permute-start.6) | collective-permute-done | bytes 360480 | tf_op jit(solution)/shard_map/ppermute | solution.py:34
  49.4 0.0 collective-permute-start.10
  49.4 0.0 collective-permute-done.9.refs_6_
  49.5 1.7 %collective-permute-done.10.refs_7_ = bf16[704,256]{1,0:T(8,128)(2,1)S(1)} collective-permute-done((bf16[704,256]{1,0:T(8,128)(2,1)S(1)}, bf16[704,256]{1,0:T(8,128)(2,1)S(1)}, u32[]{:S(2)}, u32[]{:S(2)}) %collective-permute-start.10) | collective-permute-done | bytes 360480 | tf_op jit(solution)/shard_map/ppermute | solution.py:34
  51.1 0.0 collective-permute-done.7.refs_4_
  51.1 0.0 collective-permute-done.8.refs_5_
  51.1 0.0 copy-done
  51.1 0.0 copy-done.1
  51.1 0.0 copy-done.2
  51.2 0.0 copy-done.3
  51.2 10.6 %shard_map.55 = (bf16[4,512,128]{2,1,0:T(8,128)(2,1)S(1)}, bf16[16,64,1536]{2,1,0:T(8,128)(2,1)S(1)}, bf16[16,1536,128]{2,1,0:T(8,128)(2,1)S(1)}) custom-call(s32[3,4]{1,0:T(4,128)S(1)} %copy-done.3, s32[3,1,1,2,48]{4,3,2,1,0:T(2,128)S(1)} %copy-done.2, s32[1,2,64]{2,1,0:T(2,128)S(1)} %copy-done.1, bf16[3,1,1,48,64,128]{5,4,3,2,1,0:T(8,128)(2,1)S(1)} %copy-done, ...), custom_call_target="tpu_custom_call" | custom-call | tf_op jit(solution)/shard_map/pallas_call | solution.py:218
  61.8 1.6 %collective-permute-start.11 = (bf16[4,512,128]{2,1,0:T(8,128)(2,1)S(1)}, bf16[4,512,128]{2,1,0:T(8,128)(2,1)S(1)}, u32[]{:S(2)}, u32[]{:S(2)}) collective-permute-start(bf16[4,512,128]{2,1,0:T(8,128)(2,1)S(1)} %get-tuple-element.10), channel_id=1, source_target_pairs={{0,1},{1,0},{2,3},{3,2},{4,5},{5,4},{6,7},{7,6},{8,10},{9,11},{10,... | collective-permute-start | bytes 1572872 | tf_op jit(solution)/shard_map/ppermute | solution.py:34
  63.4 2.9 %shard_map.56 = f32[4,512,128]{2,1,0:T(8,128)S(1)} custom-call(s32[1,2,64]{2,1,0:T(2,128)S(1)} %copy-done.1, bf16[16,64,1536]{2,1,0:T(8,128)(2,1)S(1)} %get-tuple-element.8.x_ref, bf16[16,1536,128]{2,1,0:T(8,128)(2,1)S(1)} %get-tuple-element.9.turned_ref), custom_call_target="tpu_custom_call" | custom-call | flops 805306368 | bytes 8388608 | tf_op jit(solution)/shard_map/pallas_call | solution.py:239
  66.4 4.7 %collective-permute-done.11 = bf16[4,512,128]{2,1,0:T(8,128)(2,1)S(1)} collective-permute-done((bf16[4,512,128]{2,1,0:T(8,128)(2,1)S(1)}, bf16[4,512,128]{2,1,0:T(8,128)(2,1)S(1)}, u32[]{:S(2)}, u32[]{:S(2)}) %collective-permute-start.11) | collective-permute-done | bytes 524320 | tf_op jit(solution)/shard_map/ppermute | solution.py:34
  71.0 0.1 convert_add_fusion
  71.2 0.9 %collective-permute-start.12 = (bf16[2,512,128]{2,1,0:T(8,128)(2,1)S(1)}, bf16[2,512,128]{2,1,0:T(8,128)(2,1)S(1)}, u32[]{:S(2)}, u32[]{:S(2)}) collective-permute-start(bf16[2,512,128]{2,1,0:T(8,128)(2,1)S(1)} %slice.37), channel_id=1, source_target_pairs={{0,2},{1,3},{2,0},{3,1},{4,6},{5,7},{6,4},{7,5},{8,9},{9,8},{10,11... | collective-permute-start | bytes 786440 | tf_op jit(solution)/shard_map/ppermute | solution.py:34
  72.1 5.5 %collective-permute-done.12 = bf16[2,512,128]{2,1,0:T(8,128)(2,1)S(1)} collective-permute-done((bf16[2,512,128]{2,1,0:T(8,128)(2,1)S(1)}, bf16[2,512,128]{2,1,0:T(8,128)(2,1)S(1)}, u32[]{:S(2)}, u32[]{:S(2)}) %collective-permute-start.12) | collective-permute-done | bytes 262176 | tf_op jit(solution)/shard_map/ppermute | solution.py:34
  77.6 0.1 slice_add_fusion
  77.7 2.2 %collective-permute-start.13 = (bf16[1,512,128]{2,1,0:T(8,128)(2,1)S(1)}, bf16[1,512,128]{2,1,0:T(8,128)(2,1)S(1)}, u32[]{:S(2)}, u32[]{:S(2)}) collective-permute-start(bf16[1,512,128]{2,1,0:T(8,128)(2,1)S(1)} %slice.38), channel_id=1, source_target_pairs={{0,4},{1,5},{2,6},{3,7},{4,0},{5,1},{6,2},{7,3},{8,12},{9,13},{10,... | collective-permute-start | bytes 393224 | tf_op jit(solution)/shard_map/ppermute | solution.py:34
  79.9 5.4 %collective-permute-done.13 = bf16[1,512,128]{2,1,0:T(8,128)(2,1)S(1)} collective-permute-done((bf16[1,512,128]{2,1,0:T(8,128)(2,1)S(1)}, bf16[1,512,128]{2,1,0:T(8,128)(2,1)S(1)}, u32[]{:S(2)}, u32[]{:S(2)}) %collective-permute-start.13) | collective-permute-done | bytes 131104 | tf_op jit(solution)/shard_map/ppermute | solution.py:34
  85.3 0.7 fusion
  (7 shorter events, 0.2 us)
Async XLA Ops:
  0.0 10.5 %collective-permute-start = (bf16[256,256]{1,0:T(8,128)(2,1)}, bf16[256,256]{1,0:T(8,128)(2,1)S(1)}, u32[]{:S(2)}, u32[]{:S(2)}) collective-permute-start(bf16[256,256]{1,0:T(8,128)(2,1)} %bitcast.1), channel_id=1, source_target_pairs={{0,4},{1,5},{2,6},{3,7},{4,0},{5,1},{6,2},{7,3},{8,12},{9,13},{10,... | collective-permute-start | bytes 393224 | tf_op jit(solution)/shard_map/ppermute | solution.py:34
  11.5 5.5 %collective-permute-start.1 = (bf16[336,256]{1,0:T(8,128)(2,1)S(1)}, bf16[336,256]{1,0:T(8,128)(2,1)S(1)}, u32[]{:S(2)}, u32[]{:S(2)}) collective-permute-start(bf16[336,256]{1,0:T(8,128)(2,1)S(1)} %pad_maximum_fusion.4), channel_id=1, source_target_pairs={{0,16},{1,17},{2,18},{3,19},{4,20},{5,21},{6,22},{7,23},{8,9},{9,8... | collective-permute-start | bytes 516104 | tf_op jit(solution)/shard_map/ppermute | solution.py:34
  17.0 34.2 %copy-start = (bf16[3,1,1,48,64,128]{5,4,3,2,1,0:T(8,128)(2,1)S(1)}, bf16[3,1,1,48,64,128]{5,4,3,2,1,0:T(8,128)(2,1)}, u32[]{:S(2)}) copy-start(bf16[3,1,1,48,64,128]{5,4,3,2,1,0:T(8,128)(2,1)} %lmat_ref.1) | copy-start | bytes 7077892
  17.0 34.2 %copy-start.1 = (s32[1,2,64]{2,1,0:T(2,128)S(1)}, s32[1,2,64]{2,1,0:T(2,128)}, u32[]{:S(2)}) copy-start(s32[1,2,64]{2,1,0:T(2,128)} %ex_hbm.3) | copy-start | bytes 1540
  17.0 34.2 %copy-start.2 = (s32[3,1,1,2,48]{4,3,2,1,0:T(2,128)S(1)}, s32[3,1,1,2,48]{4,3,2,1,0:T(2,128)}, u32[]{:S(2)}) copy-start(s32[3,1,1,2,48]{4,3,2,1,0:T(2,128)} %lists_hbm.1) | copy-start | bytes 3460
  17.0 34.2 %copy-start.3 = (s32[3,4]{1,0:T(4,128)S(1)}, s32[3,4]{1,0:T(4,128)}, u32[]{:S(2)}) copy-start(s32[3,4]{1,0:T(4,128)} %match_hbm.1) | copy-start | bytes 148
  17.0 7.3 %collective-permute-start.2 = (bf16[672,256]{1,0:T(8,128)(2,1)S(1)}, bf16[672,256]{1,0:T(8,128)(2,1)S(1)}, u32[]{:S(2)}, u32[]{:S(2)}) collective-permute-start(bf16[672,256]{1,0:T(8,128)(2,1)S(1)} %pad_maximum_fusion.2), channel_id=1, source_target_pairs={{0,1},{1,0},{2,3},{3,2},{4,5},{5,4},{6,7},{7,6},{8,10},{9,11},{10,... | collective-permute-start | bytes 1032200 | tf_op jit(solution)/shard_map/ppermute | solution.py:34
  24.4 19.2 %collective-permute-start.3 = (bf16[1344,256]{1,0:T(8,128)(2,1)S(1)}, bf16[1344,256]{1,0:T(8,128)(2,1)S(1)}, u32[]{:S(2)}, u32[]{:S(2)}) collective-permute-start(bf16[1344,256]{1,0:T(8,128)(2,1)S(1)} %pad_maximum_fusion.refs_0_), channel_id=1, source_target_pairs={{0,2},{1,3},{2,0},{3,1},{4,6},{5,7},{6,4},{7,5},{8,24},{9,25},{10,... | collective-permute-start | bytes 2064392 | tf_op jit(solution)/shard_map/ppermute | solution.py:34
  25.3 11.1 %collective-permute-start.4 = (bf16[176,256]{1,0:T(8,128)(2,1)S(1)}, bf16[176,256]{1,0:T(8,128)(2,1)S(1)}, u32[]{:S(2)}, u32[]{:S(2)}) collective-permute-start(bf16[176,256]{1,0:T(8,128)(2,1)S(1)} %slice.26), channel_id=1, source_target_pairs={{0,2},{1,3},{2,0},{3,1},{4,6},{5,7},{6,4},{7,5},{8,10},{9,11},{10,... | collective-permute-start | bytes 270344 | tf_op jit(solution)/shard_map/ppermute | solution.py:34
  36.4 5.6 %collective-permute-start.5 = (bf16[352,256]{1,0:T(8,128)(2,1)S(1)}, bf16[352,256]{1,0:T(8,128)(2,1)S(1)}, u32[]{:S(2)}, u32[]{:S(2)}) collective-permute-start(bf16[352,256]{1,0:T(8,128)(2,1)S(1)} %pad_maximum_fusion.3), channel_id=1, source_target_pairs={{0,16},{1,17},{2,18},{3,19},{4,20},{5,21},{6,22},{7,23},{8,24},{9,... | collective-permute-start | bytes 540680 | tf_op jit(solution)/shard_map/ppermute | solution.py:34
  42.0 7.5 %collective-permute-start.6 = (bf16[704,256]{1,0:T(8,128)(2,1)S(1)}, bf16[704,256]{1,0:T(8,128)(2,1)S(1)}, u32[]{:S(2)}, u32[]{:S(2)}) collective-permute-start(bf16[704,256]{1,0:T(8,128)(2,1)S(1)} %pad_maximum_fusion.1.refs_2_), channel_id=1, source_target_pairs={{0,1},{1,0},{2,3},{3,2},{4,5},{5,4},{6,7},{7,6},{8,9},{9,8},{10,11... | collective-permute-start | bytes 1081352 | tf_op jit(solution)/shard_map/ppermute | solution.py:34
  43.6 7.5 %collective-permute-start.7 = (bf16[1344,256]{1,0:T(8,128)(2,1)S(1)}, bf16[1344,256]{1,0:T(8,128)(2,1)S(1)}, u32[]{:S(2)}, u32[]{:S(2)}) collective-permute-start(bf16[1344,256]{1,0:T(8,128)(2,1)S(1)} %pad_maximum_fusion.refs_0_), channel_id=1, source_target_pairs={{0,8},{1,9},{2,10},{3,11},{4,12},{5,13},{6,14},{7,15},{8,0},{9,1},... | collective-permute-start | bytes 2064392 | tf_op jit(solution)/shard_map/ppermute | solution.py:34
  43.6 7.5 %collective-permute-start.8 = (bf16[1344,256]{1,0:T(8,128)(2,1)S(1)}, bf16[1344,256]{1,0:T(8,128)(2,1)S(1)}, u32[]{:S(2)}, u32[]{:S(2)}) collective-permute-start(bf16[1344,256]{1,0:T(8,128)(2,1)S(1)} %collective-permute-done.3.refs_1_), channel_id=1, source_target_pairs={{0,8},{1,9},{2,10},{3,11},{4,12},{5,13},{6,14},{7,15},{8,0},{9,1},... | collective-permute-start | bytes 2064392 | tf_op jit(solution)/shard_map/ppermute | solution.py:34
  44.1 5.3 %collective-permute-start.9 = (bf16[704,256]{1,0:T(8,128)(2,1)S(1)}, bf16[704,256]{1,0:T(8,128)(2,1)S(1)}, u32[]{:S(2)}, u32[]{:S(2)}) collective-permute-start(bf16[704,256]{1,0:T(8,128)(2,1)S(1)} %pad_maximum_fusion.1.refs_2_), channel_id=1, source_target_pairs={{0,8},{1,9},{2,10},{3,11},{4,12},{5,13},{6,14},{7,15},{8,0},{9,1},... | collective-permute-start | bytes 1081352 | tf_op jit(solution)/shard_map/ppermute | solution.py:34
  49.4 1.7 %collective-permute-start.10 = (bf16[704,256]{1,0:T(8,128)(2,1)S(1)}, bf16[704,256]{1,0:T(8,128)(2,1)S(1)}, u32[]{:S(2)}, u32[]{:S(2)}) collective-permute-start(bf16[704,256]{1,0:T(8,128)(2,1)S(1)} %collective-permute-done.6.refs_3_), channel_id=1, source_target_pairs={{0,8},{1,9},{2,10},{3,11},{4,12},{5,13},{6,14},{7,15},{8,0},{9,1},... | collective-permute-start | bytes 1081352 | tf_op jit(solution)/shard_map/ppermute | solution.py:34
  61.8 9.2 %collective-permute-start.11 = (bf16[4,512,128]{2,1,0:T(8,128)(2,1)S(1)}, bf16[4,512,128]{2,1,0:T(8,128)(2,1)S(1)}, u32[]{:S(2)}, u32[]{:S(2)}) collective-permute-start(bf16[4,512,128]{2,1,0:T(8,128)(2,1)S(1)} %get-tuple-element.10), channel_id=1, source_target_pairs={{0,1},{1,0},{2,3},{3,2},{4,5},{5,4},{6,7},{7,6},{8,10},{9,11},{10,... | collective-permute-start | bytes 1572872 | tf_op jit(solution)/shard_map/ppermute | solution.py:34
  71.2 6.4 %collective-permute-start.12 = (bf16[2,512,128]{2,1,0:T(8,128)(2,1)S(1)}, bf16[2,512,128]{2,1,0:T(8,128)(2,1)S(1)}, u32[]{:S(2)}, u32[]{:S(2)}) collective-permute-start(bf16[2,512,128]{2,1,0:T(8,128)(2,1)S(1)} %slice.37), channel_id=1, source_target_pairs={{0,2},{1,3},{2,0},{3,1},{4,6},{5,7},{6,4},{7,5},{8,9},{9,8},{10,11... | collective-permute-start | bytes 786440 | tf_op jit(solution)/shard_map/ppermute | solution.py:34
  77.7 7.6 %collective-permute-start.13 = (bf16[1,512,128]{2,1,0:T(8,128)(2,1)S(1)}, bf16[1,512,128]{2,1,0:T(8,128)(2,1)S(1)}, u32[]{:S(2)}, u32[]{:S(2)}) collective-permute-start(bf16[1,512,128]{2,1,0:T(8,128)(2,1)S(1)} %slice.38), channel_id=1, source_target_pairs={{0,4},{1,5},{2,6},{3,7},{4,0},{5,1},{6,2},{7,3},{8,12},{9,13},{10,... | collective-permute-start | bytes 393224 | tf_op jit(solution)/shard_map/ppermute | solution.py:34
where the time goes:
time: 86.2 us; the launch traced here: 86 us
  waiting for transfers between devices  52.5 us (61%)
  starting transfers between devices  17.9 us (21%)
  Pallas kernels  13.5 us (16%)
  other arithmetic  1.9 us (2%)
    ppermute x14, waiting for transfers between devices, swap_by(): return lax.ppermute(arr, AXES, perm)  52.5 us
    ppermute x14, starting transfers between devices, swap_by(): return lax.ppermute(arr, AXES, perm)  17.9 us
    pallas_call x1, Pallas kernels, on_device(): pl.pallas_call(functools.partial(half_kernel, nka, nfit, nq, nblk, edge,...  10.6 us
    pallas_call x1, Pallas kernels, on_device(): pl.pallas_call(functools.partial(rest_kernel, nfit, edge), out_shape=jax....  2.92 us
  transfers between devices with their start and end apart: 14, of which 10 were waited for; matrix products, arithmetic and copies ran while one was open for 0% of the time, Pallas kernels for 3%

commit v1 on v0

v1 whole, which is shorter than its diff:
```python
import functools

import jax
import jax.numpy as jnp
from jax import lax
from jax.experimental import pallas as pl
from jax.experimental.pallas import tpu as pltpu
from jax.sharding import PartitionSpec as P

AXES = ("ka", "fit")


def bits_of(size):
    return [1 << b for b in range(size.bit_length() - 1)]


def swap_by(arr, nka, nfit, dka, dfit):
    perm = [
        (k * nfit + f, (k ^ dka) * nfit + (f ^ dfit)) for k in range(nka) for f in range(nfit)
    ]
    return lax.ppermute(arr, AXES, perm)


def far_offsets(nfit):
    offsets = [0]
    for bit in bits_of(nfit)[2:]:
        offsets = offsets + [o ^ bit for o in offsets]
    return offsets


def gather_shards(shard, nka, nfit):
    half, core = nka // 2, 1
    y, w = bits_of(nfit)[:2]
    size = shard.size // shard.shape[-1]

    def swap(arr, dka, dfit):
        return swap_by(arr, nka, nfit, dka, dfit)

    def join(*arrs):
        return jnp.concatenate(arrs, axis=0)

    own = shard.reshape(size, shard.shape[-1])
    bits = bits_of(nfit)[2:]
    near = both = own
    for bit in bits[:-1]:
        near = both = join(both, swap(both, 0, bit))
    far, x_near, y_near, xy_near = lax.optimization_barrier(
        (
            swap(near, 0, bits[-1]),
            swap(near, half, 0),
            swap(near, 0, y),
            swap(near, half, y),
        )
    )
    both = join(near, far)
    w_both, x_far, y_far, xy_far = lax.optimization_barrier(
        (swap(both, 0, w), swap(far, half, 0), swap(far, 0, y), swap(far, half, y))
    )
    xy_both = join(xy_near, xy_far)
    xw_both, yw_both, xyw_both = lax.optimization_barrier(
        (swap(w_both, half, 0), swap(w_both, 0, y), swap(xy_both, 0, w))
    )
    held = [
        ((0, 0), both),
        ((half, 0), join(x_near, x_far)),
        ((0, y), join(y_near, y_far)),
        ((half, y), xy_both),
        ((0, w), w_both),
        ((half, w), xw_both),
        ((0, y | w), yw_both),
        ((half, y | w), xyw_both),
    ]
    held = held + [((dka ^ core, dfit), swap(arr, core, 0)) for (dka, dfit), arr in held]
    return [off for off, _ in held], [arr for _, arr in held]


def exchange_units(owner_of, second, unit, edge, x_ref, turned_ref, ex_ref, out_ref):
    count, rows, _ = out_ref.shape
    for slot in range(count):
        for step in range(rows // unit):
            row = owner_of(slot) * (2 * rows) + second * rows + step * unit
            e = row // edge
            lb, rb = ex_ref[0, 0, e], ex_ref[0, 1, e]
            lo = pl.multiple_of(lax.rem(row, edge), unit)
            out_ref[slot, step * unit : (step + 1) * unit, :] = jnp.dot(
                x_ref[lb, pl.ds(lo, unit), :],
                turned_ref[rb],
                preferred_element_type=jnp.float32,
            ).astype(out_ref.dtype)


def chunk_owner(offs):
    fit = lax.axis_index("fit")
    return lambda slot: lax.bitwise_xor(fit, offs[slot])


def half_kernel(
    offsets, far, orders, nq, nblk, edge, occ, nbl, rows, match_hbm, lists_hbm, ex_hbm, lmat_ref, *refs
):
    held = refs[: len(offsets)]
    first_ref, second_ref, x_ref, turned_ref = refs[len(offsets) : len(offsets) + 4]
    match_ref, lists_ref, ex_ref, l_ref, ops_ref, sums_ref, sems, small = refs[len(offsets) + 4 :]
    ka, fit = lax.axis_index("ka"), lax.axis_index("fit")
    sub = min(rows, edge)
    loads = [
        pltpu.make_async_copy(src, dst, small.at[i])
        for i, (src, dst) in enumerate(
            [(match_hbm, match_ref), (lists_hbm, lists_ref), (ex_hbm, ex_ref)]
        )
    ]
    copies = [
        pltpu.make_async_copy(lmat_ref.at[qq, 0, 0], l_ref.at[qq], sems.at[qq]) for qq in range(nq)
    ]
    for copy in loads + copies:
        copy.start()
    for copy in loads:
        copy.wait()

    def place(ref, owner):
        for row in range(0, ref.shape[0], sub):
            piece, rest = divmod(row, 2 * rows)
            part, inner = divmod(rest, rows)
            start = lax.bitwise_xor(owner, far[piece]) * rows + inner
            dst = (start // edge) * (2 * edge) + lax.rem(start, edge)
            dst = pl.multiple_of(dst, sub)
            low = pl.multiple_of(dst + edge, sub)
            value = ref[row : row + sub, :]
            if part == 0:
                ops_ref[pl.ds(dst, sub), :occ] = value
                ops_ref[pl.ds(low, sub), occ:] = value
            else:
                ops_ref[pl.ds(dst, sub), occ:] = value
                ops_ref[pl.ds(low, sub), :occ] = -value

    for qq in range(nq):
        want = lax.bitwise_xor(match_ref[qq, ka], ka)
        for dka in sorted({off[0] for off in offsets}):

            @pl.when(want == dka)
            def _():
                for off, ref in zip(offsets, held):
                    if off[0] == dka:
                        place(ref, lax.bitwise_xor(fit, off[1]))

        sums_ref[...] = jnp.zeros_like(sums_ref)
        copies[qq].wait()

        def one_block(n, c):
            rb = pl.multiple_of(lists_ref[qq, 0, 0, 0, n] * edge, edge)
            cb = pl.multiple_of(lists_ref[qq, 0, 0, 1, n] * (2 * edge), 2 * edge)
            sums_ref[pl.ds(rb, edge), :] += jnp.dot(
                l_ref[qq, n],
                ops_ref[pl.ds(cb, 2 * edge), :],
                preferred_element_type=jnp.float32,
            )
            return c

        lax.fori_loop(0, nblk, one_block, 0, unroll=16)

        def one_row(rb, c):
            x = sums_ref[pl.ds(pl.multiple_of(rb * edge, edge), edge), :].astype(jnp.bfloat16)
            x_ref[rb, :, qq * 2 * occ : (qq + 1) * 2 * occ] = x
            low = jnp.concatenate([-x[:, occ:], x[:, :occ]], axis=1)
            turned_ref[rb, qq * 2 * occ : (qq + 1) * 2 * occ, :] = jnp.concatenate([x, low], axis=0).T
            return c

        lax.fori_loop(0, nbl, one_row, 0, unroll=4)

    unit = min(edge, first_ref.shape[1])
    for second, ref in enumerate((first_ref, second_ref)):
        exchange_units(chunk_owner(orders[second]), second, unit, edge, x_ref, turned_ref, ex_ref, ref)


def rest_kernel(orders, edge, ex_hbm, x_ref, turned_ref, first_ref, second_ref, ex_ref, sem):
    copy = pltpu.make_async_copy(ex_hbm, ex_ref, sem)
    copy.start()
    copy.wait()
    unit = min(edge, first_ref.shape[1])
    for second, ref in enumerate((first_ref, second_ref)):
        exchange_units(chunk_owner(orders[second]), second, unit, edge, x_ref, turned_ref, ex_ref, ref)


def on_device(nka, nfit, integrals, block_lists, coeff, match, ex_blocks):
    nq, _, _, nblk, edge, _ = integrals.shape
    rows, occ = coeff.shape[2:]
    nexch = ex_blocks.shape[2]
    nbl = nfit * rows // edge
    offsets, held = gather_shards(coeff, nka, nfit)
    vmem = pl.BlockSpec(memory_space=pltpu.VMEM)
    hbm = pl.BlockSpec(memory_space=pltpu.HBM)
    params = pltpu.CompilerParams(vmem_limit_bytes=28 * 1024 * 1024)
    bf16, f32, i32 = jnp.bfloat16, jnp.float32, jnp.int32

    bits, far = bits_of(nfit), far_offsets(nfit)
    y, w = bits[:2]
    keep_a = far + [o ^ w for o in far]
    keep_b = far + [o ^ y for o in far]
    send_a = [o ^ y for o in keep_a]
    send_b = [o ^ w for o in keep_b]
    count, half = nfit // 2, nexch * edge // nfit // 2
    out_a, out_b, xmat, turned = pl.pallas_call(
        functools.partial(
            half_kernel, offsets, far, (send_a, send_b), nq, nblk, edge, occ, nbl, rows
        ),
        out_shape=[jax.ShapeDtypeStruct((count, half, 2 * edge), bf16)] * 2
        + [
            jax.ShapeDtypeStruct((nbl, edge, nq * 2 * occ), bf16),
            jax.ShapeDtypeStruct((nbl, nq * 2 * occ, 2 * edge), bf16),
        ],
        in_specs=[hbm] * 4 + [vmem] * len(held),
        out_specs=[vmem] * 4,
        scratch_shapes=[
            pltpu.SMEM(match.shape, i32),
            pltpu.SMEM(block_lists.shape, i32),
            pltpu.SMEM(ex_blocks.shape, i32),
            pltpu.VMEM((nq, nblk, edge, 2 * edge), bf16),
            pltpu.VMEM((nbl * 2 * edge, 2 * occ), bf16),
            pltpu.VMEM((nbl * edge, 2 * occ), f32),
            pltpu.SemaphoreType.DMA((nq,)),
            pltpu.SemaphoreType.DMA((3,)),
        ],
        compiler_params=params,
    )(match, block_lists, ex_blocks, integrals, *held)
    own_a, own_b = pl.pallas_call(
        functools.partial(rest_kernel, (keep_a, keep_b), edge),
        out_shape=[jax.ShapeDtypeStruct((count, half, 2 * edge), f32)] * 2,
        in_specs=[hbm, vmem, vmem],
        out_specs=[vmem] * 2,
        scratch_shapes=[pltpu.SMEM(ex_blocks.shape, i32), pltpu.SemaphoreType.DMA],
        compiler_params=params,
        cost_estimate=pl.CostEstimate(
            flops=nexch * edge * edge * 2 * nq * 2 * occ, bytes_accessed=1 << 23, transcendentals=0
        ),
    )(ex_blocks, xmat, turned)

    def swap(arr, dfit):
        return swap_by(arr, nka, nfit, 0, dfit)

    n = count // 2
    sum_a = own_a + swap(out_a, y).astype(f32)
    sum_b = own_b + swap(out_b, w).astype(f32)
    got_a = swap(sum_a[n:].astype(bf16), w)
    got_b = swap(sum_b[n:].astype(bf16), y)
    total = jnp.concatenate(
        [sum_a[:n] + got_a.astype(f32), sum_b[:n] + got_b.astype(f32)], axis=1
    )
    for bit in bits[:1:-1]:
        n = n // 2
        total = total[:n] + swap(total[n:].astype(bf16), bit).astype(f32)
    factor = -((nq * nfit * occ) ** (-0.5))
    return total * factor


def solution(mesh):
    nka, nfit = mesh.shape["ka"], mesh.shape["fit"]
    return jax.shard_map(
        functools.partial(on_device, nka, nfit),
        mesh=mesh,
        in_specs=(
            P(None, "ka", "fit", None, None, None),
            P(None, "ka", "fit", None, None),
            P("ka", None, "fit", None),
            P(),
            P("ka", None, None),
        ),
        out_specs=P("ka", "fit", None),
        check_vma=False,
    )
```

time: 86.2 us -> 73.1 us (0.85)
  waiting for transfers between devices: 52.5 us -> 29.6 us
  starting transfers between devices: 17.9 us -> 24.5 us
  local copies, waits for them, and re-layouts: 0.08 us -> 3.81 us
    ppermute x14 -> x24, waiting for transfers between devices: 52.5 us -> 29.6 us  [swap_by(): return lax.ppermute(arr, AXES, perm)]
    ppermute x14 -> x24, starting transfers between devices: 17.9 us -> 24.5 us  [swap_by(): return lax.ppermute(arr, AXES, perm)]
    unnamed x8 -> x13, local copies, waits for them, and re-layouts: 0.03 us -> 3.74 us
  transfers between devices with their start and end apart: 14 -> 24, of which waited for: 10 -> 18; matrix products, arithmetic and copies ran while one was open for 0% -> 0% of each run, Pallas kernels for 3% -> 4%
where the time goes in v1:
time: 73.1 us; the launch traced here: 72.9 us
  waiting for transfers between devices  29.6 us (40%)
  starting transfers between devices  24.5 us (34%)
  Pallas kernels  13 us (18%)
  local copies, waits for them, and re-layouts  3.81 us (5%)
  other arithmetic  1.84 us (3%)
    ppermute x24, waiting for transfers between devices, swap_by(): return lax.ppermute(arr, AXES, perm)  29.6 us
    ppermute x24, starting transfers between devices, swap_by(): return lax.ppermute(arr, AXES, perm)  24.5 us
    pallas_call x1, Pallas kernels, on_device(): pl.pallas_call(functools.partial(half_kernel, offsets, far, (send_a, send...  10.1 us
    unnamed x13, local copies, waits for them, and re-layouts  3.74 us
    pallas_call x1, Pallas kernels, on_device(): pl.pallas_call(functools.partial(rest_kernel, (keep_a, keep_b), edge), ou...  2.93 us
  transfers between devices with their start and end apart: 24, of which 18 were waited for; matrix products, arithmetic and copies ran while one was open for 0% of the time, Pallas kernels for 4%

profile of v1, /device:TPU:0, one launch (start us, length us, event | category | flops | bytes accessed | tf_op | source)
XLA Modules:
  0.0 72.9 jit_solution(10753410871394385361)
XLA Ops:
  0.0 3.9 %collective-permute-start.3 = (bf16[256,256]{1,0:T(8,128)(2,1)}, bf16[256,256]{1,0:T(8,128)(2,1)S(1)}, u32[]{:S(2)}, u32[]{:S(2)}) collective-permute-start(bf16[256,256]{1,0:T(8,128)(2,1)} %bitcast.1), channel_id=1, source_target_pairs={{0,17},{1,16},{2,19},{3,18},{4,21},{5,20},{6,23},{7,22},{8,25},{9,... | collective-permute-start | bytes 393224 | tf_op jit(solution)/shard_map/ppermute | solution.py:21
  3.9 0.5 collective-permute-start.2
  4.5 3.1 %collective-permute-start = (bf16[256,256]{1,0:T(8,128)(2,1)}, bf16[256,256]{1,0:T(8,128)(2,1)S(1)}, u32[]{:S(2)}, u32[]{:S(2)}) collective-permute-start(bf16[256,256]{1,0:T(8,128)(2,1)} %bitcast.4), channel_id=1, source_target_pairs={{0,4},{1,5},{2,6},{3,7},{4,0},{5,1},{6,2},{7,3},{8,12},{9,13},{10,... | collective-permute-start | bytes 393224 | tf_op jit(solution)/shard_map/ppermute | solution.py:21
  7.5 0.6 collective-permute-done.3
  8.1 2.3 %collective-permute-done.2 = bf16[256,256]{1,0:T(8,128)(2,1)S(1)} collective-permute-done((bf16[256,256]{1,0:T(8,128)(2,1)}, bf16[256,256]{1,0:T(8,128)(2,1)S(1)}, u32[]{:S(2)}, u32[]{:S(2)}) %collective-permute-start.2) | collective-permute-done | bytes 131104 | tf_op jit(solution)/shard_map/ppermute | solution.py:21
  10.4 0.3 collective-permute-done.1
  10.7 2.6 %collective-permute-done = bf16[256,256]{1,0:T(8,128)(2,1)S(1)} collective-permute-done((bf16[256,256]{1,0:T(8,128)(2,1)}, bf16[256,256]{1,0:T(8,128)(2,1)S(1)}, u32[]{:S(2)}, u32[]{:S(2)}) %collective-permute-start) | collective-permute-done | bytes 131104 | tf_op jit(solution)/shard_map/ppermute | solution.py:21
  13.2 0.9 %pad_maximum_fusion.1.refs_0_ = bf16[512,256]{1,0:T(8,128)(2,1)S(1)} fusion(bf16[256,256]{1,0:T(8,128)(2,1)S(1)} %collective-permute-done, bf16[256,256]{1,0:T(8,128)(2,1)} %bitcast.5), kind=kLoop, calls=%fused_computation.13 | loop fusion | flops 524288 | bytes 524288 | tf_op jit(solution)/shard_map/concatenate | solution.py:40
  14.2 0.9 %collective-permute-start.4 = (bf16[512,256]{1,0:T(8,128)(2,1)S(1)}, bf16[512,256]{1,0:T(8,128)(2,1)S(1)}, u32[]{:S(2)}, u32[]{:S(2)}) collective-permute-start(bf16[512,256]{1,0:T(8,128)(2,1)S(1)} %pad_maximum_fusion.1.refs_0_), channel_id=1, source_target_pairs={{0,2},{1,3},{2,0},{3,1},{4,6},{5,7},{6,4},{7,5},{8,10},{9,11},{10,... | collective-permute-start | bytes 786440 | tf_op jit(solution)/shard_map/ppermute | solution.py:21
  15.0 2.4 %collective-permute-start.7 = (bf16[256,256]{1,0:T(8,128)(2,1)S(1)}, bf16[256,256]{1,0:T(8,128)(2,1)S(1)}, u32[]{:S(2)}, u32[]{:S(2)}) collective-permute-start(bf16[256,256]{1,0:T(8,128)(2,1)S(1)} %collective-permute-done), channel_id=1, source_target_pairs={{0,17},{1,16},{2,19},{3,18},{4,21},{5,20},{6,23},{7,22},{8,25},{9,... | collective-permute-start | bytes 393224 | tf_op jit(solution)/shard_map/ppermute | solution.py:21
  17.5 0.5 collective-permute-start.6
  18.0 0.5 collective-permute-start.5
  18.5 3.2 %collective-permute-done.7 = bf16[256,256]{1,0:T(8,128)(2,1)S(1)} collective-permute-done((bf16[256,256]{1,0:T(8,128)(2,1)S(1)}, bf16[256,256]{1,0:T(8,128)(2,1)S(1)}, u32[]{:S(2)}, u32[]{:S(2)}) %collective-permute-start.7) | collective-permute-done | bytes 131104 | tf_op jit(solution)/shard_map/ppermute | solution.py:21
  21.8 1.5 %collective-permute-done.6 = bf16[256,256]{1,0:T(8,128)(2,1)S(1)} collective-permute-done((bf16[256,256]{1,0:T(8,128)(2,1)S(1)}, bf16[256,256]{1,0:T(8,128)(2,1)S(1)}, u32[]{:S(2)}, u32[]{:S(2)}) %collective-permute-start.6) | collective-permute-done | bytes 131104 | tf_op jit(solution)/shard_map/ppermute | solution.py:21
  23.2 0.1 collective-permute-done.5
  23.3 1.1 %collective-permute-start.10 = (bf16[512,256]{1,0:T(8,128)(2,1)S(1)}, bf16[512,256]{1,0:T(8,128)(2,1)S(1)}, u32[]{:S(2)}, u32[]{:S(2)}) collective-permute-start(bf16[512,256]{1,0:T(8,128)(2,1)S(1)} %constant_dynamic-update-slice_fusion.4.refs_3_), channel_id=1, source_target_pairs={{0,2},{1,3},{2,0},{3,1},{4,6},{5,7},{6,4},{7,5},{8,10},{9,11},{10,... | collective-permute-start | bytes 786440 | tf_op jit(solution)/shard_map/ppermute | solution.py:21
  24.4 1.5 %collective-permute-start.9 = (bf16[512,256]{1,0:T(8,128)(2,1)S(1)}, bf16[512,256]{1,0:T(8,128)(2,1)S(1)}, u32[]{:S(2)}, u32[]{:S(2)}) collective-permute-start(bf16[512,256]{1,0:T(8,128)(2,1)S(1)} %collective-permute-done.4.refs_4_), channel_id=1, source_target_pairs={{0,1},{1,0},{2,3},{3,2},{4,5},{5,4},{6,7},{7,6},{8,9},{9,8},{10,11... | collective-permute-start | bytes 786440 | tf_op jit(solution)/shard_map/ppermute | solution.py:21
  25.9 0.5 collective-permute-start.8
  26.4 0.1 collective-permute-start.13
  26.6 4.0 %collective-permute-done.10.refs_7_ = bf16[512,256]{1,0:T(8,128)(2,1)S(1)} collective-permute-done((bf16[512,256]{1,0:T(8,128)(2,1)S(1)}, bf16[512,256]{1,0:T(8,128)(2,1)S(1)}, u32[]{:S(2)}, u32[]{:S(2)}) %collective-permute-start.10) | collective-permute-done | bytes 262176 | tf_op jit(solution)/shard_map/ppermute | solution.py:21
  30.6 0.3 collective-permute-done.9.refs_6_
  30.9 0.3 collective-permute-start.14
  31.1 1.2 %collective-permute-done.8.refs_5_ = bf16[512,256]{1,0:T(8,128)(2,1)S(1)} collective-permute-done((bf16[512,256]{1,0:T(8,128)(2,1)S(1)}, bf16[512,256]{1,0:T(8,128)(2,1)S(1)}, u32[]{:S(2)}, u32[]{:S(2)}) %collective-permute-start.8) | collective-permute-done | bytes 262176 | tf_op jit(solution)/shard_map/ppermute | solution.py:21
  32.3 0.5 collective-permute-start.16
  32.8 0.1 collective-permute-start.17
  32.9 0.4 collective-permute-start.18
  33.3 0.5 collective-permute-done.15.refs_12_
  33.8 0.4 collective-permute-done.16.refs_13_
  34.2 0.4 collective-permute-done.17.refs_14_
  34.5 0.4 collective-permute-done.18.refs_15_
  34.9 1.7 %copy-done = bf16[3,1,1,48,64,128]{5,4,3,2,1,0:T(8,128)(2,1)S(1)} copy-done((bf16[3,1,1,48,64,128]{5,4,3,2,1,0:T(8,128)(2,1)S(1)}, bf16[3,1,1,48,64,128]{5,4,3,2,1,0:T(8,128)(2,1)}, u32[]{:S(2)}) %copy-start) | copy-done | bytes 2359320
  36.6 0.7 copy-done.1
  37.3 0.7 copy-done.3
  38.0 0.7 copy-done.4
  38.6 10.1 %shard_map.55 = (bf16[4,256,128]{2,1,0:T(8,128)(2,1)S(1)}, bf16[4,256,128]{2,1,0:T(8,128)(2,1)S(1)}, bf16[16,64,1536]{2,1,0:T(8,128)(2,1)S(1)}, bf16[16,1536,128]{2,1,0:T(8,128)(2,1)S(1)}) custom-call(s32[3,4]{1,0:T(4,128)S(1)} %copy-done.4, s32[3,1,1,2,48]{4,3,2,1,0:T(2,128)S(1)} %copy-done.3, s32[1,2,64]{2,1,0:T(2,128)S(1)} %copy-done.1, ...), custom_call_target="tpu_custom_call" | custom-call | tf_op jit(solution)/shard_map/pallas_call | solution.py:201
  48.8 1.0 %collective-permute-start.19 = (bf16[4,256,128]{2,1,0:T(8,128)(2,1)S(1)}, bf16[4,256,128]{2,1,0:T(8,128)(2,1)S(1)}, u32[]{:S(2)}, u32[]{:S(2)}) collective-permute-start(bf16[4,256,128]{2,1,0:T(8,128)(2,1)S(1)} %get-tuple-element.36), channel_id=1, source_target_pairs={{0,1},{1,0},{2,3},{3,2},{4,5},{5,4},{6,7},{7,6},{8,9},{9,8},{10,11... | collective-permute-start | bytes 786440 | tf_op jit(solution)/shard_map/ppermute | solution.py:21
  49.7 1.4 %collective-permute-start.21 = (bf16[4,256,128]{2,1,0:T(8,128)(2,1)S(1)}, bf16[4,256,128]{2,1,0:T(8,128)(2,1)S(1)}, u32[]{:S(2)}, u32[]{:S(2)}) collective-permute-start(bf16[4,256,128]{2,1,0:T(8,128)(2,1)S(1)} %get-tuple-element.38), channel_id=1, source_target_pairs={{0,2},{1,3},{2,0},{3,1},{4,6},{5,7},{6,4},{7,5},{8,10},{9,11},{10,... | collective-permute-start | bytes 786440 | tf_op jit(solution)/shard_map/ppermute | solution.py:21
  51.1 2.9 %shard_map.56 = (f32[4,256,128]{2,1,0:T(8,128)S(1)}, f32[4,256,128]{2,1,0:T(8,128)S(1)}) custom-call(s32[1,2,64]{2,1,0:T(2,128)S(1)} %copy-done.2, bf16[16,64,1536]{2,1,0:T(8,128)(2,1)S(1)} %get-tuple-element.33.x_ref, bf16[16,1536,128]{2,1,0:T(8,128)(2,1)S(1)} %get-tuple-element.34.turned_ref), custom_call_target="tpu_custom_call" | custom-call | flops 805306368 | bytes 8388608 | tf_op jit(solution)/shard_map/pallas_call | solution.py:224
  54.1 3.1 %collective-permute-done.19 = bf16[4,256,128]{2,1,0:T(8,128)(2,1)S(1)} collective-permute-done((bf16[4,256,128]{2,1,0:T(8,128)(2,1)S(1)}, bf16[4,256,128]{2,1,0:T(8,128)(2,1)S(1)}, u32[]{:S(2)}, u32[]{:S(2)}) %collective-permute-start.19) | collective-permute-done | bytes 262176 | tf_op jit(solution)/shard_map/ppermute | solution.py:21
  57.2 0.1 convert_add_fusion.1
  57.3 1.7 %collective-permute-start.20 = (bf16[2,256,128]{2,1,0:T(8,128)(2,1)S(1)}, bf16[2,256,128]{2,1,0:T(8,128)(2,1)S(1)}, u32[]{:S(2)}, u32[]{:S(2)}) collective-permute-start(bf16[2,256,128]{2,1,0:T(8,128)(2,1)S(1)} %slice.48), channel_id=1, source_target_pairs={{0,2},{1,3},{2,0},{3,1},{4,6},{5,7},{6,4},{7,5},{8,10},{9,11},{10,... | collective-permute-start | bytes 393224 | tf_op jit(solution)/shard_map/ppermute | solution.py:21
  59.0 0.1 convert_add_fusion
  59.1 0.7 collective-permute-start.22
  59.8 2.5 %collective-permute-done.20 = bf16[2,256,128]{2,1,0:T(8,128)(2,1)S(1)} collective-permute-done((bf16[2,256,128]{2,1,0:T(8,128)(2,1)S(1)}, bf16[2,256,128]{2,1,0:T(8,128)(2,1)S(1)}, u32[]{:S(2)}, u32[]{:S(2)}) %collective-permute-start.20) | collective-permute-done | bytes 131104 | tf_op jit(solution)/shard_map/ppermute | solution.py:21
  62.3 1.8 %collective-permute-done.22 = bf16[2,256,128]{2,1,0:T(8,128)(2,1)S(1)} collective-permute-done((bf16[2,256,128]{2,1,0:T(8,128)(2,1)S(1)}, bf16[2,256,128]{2,1,0:T(8,128)(2,1)S(1)}, u32[]{:S(2)}, u32[]{:S(2)}) %collective-permute-start.22) | collective-permute-done | bytes 131104 | tf_op jit(solution)/shard_map/ppermute | solution.py:21
  64.2 3.3 %collective-permute-start.23 = (bf16[1,512,128]{2,1,0:T(8,128)(2,1)S(1)}, bf16[1,512,128]{2,1,0:T(8,128)(2,1)S(1)}, u32[]{:S(2)}, u32[]{:S(2)}) collective-permute-start(bf16[1,512,128]{2,1,0:T(8,128)(2,1)S(1)} %fusion.3), channel_id=1, source_target_pairs={{0,4},{1,5},{2,6},{3,7},{4,0},{5,1},{6,2},{7,3},{8,12},{9,13},{10,... | collective-permute-start | bytes 393224 | tf_op jit(solution)/shard_map/ppermute | solution.py:21
  67.5 4.7 %collective-permute-done.23 = bf16[1,512,128]{2,1,0:T(8,128)(2,1)S(1)} collective-permute-done((bf16[1,512,128]{2,1,0:T(8,128)(2,1)S(1)}, bf16[1,512,128]{2,1,0:T(8,128)(2,1)S(1)}, u32[]{:S(2)}, u32[]{:S(2)}) %collective-permute-start.23) | collective-permute-done | bytes 131104 | tf_op jit(solution)/shard_map/ppermute | solution.py:21
  72.2 0.7 %fusion.2 = f32[1,512,128]{2,1,0:T(8,128)} fusion(f32[2,256,128]{2,1,0:T(8,128)S(1)} %slice_add_fusion.1, f32[2,256,128]{2,1,0:T(8,128)S(1)} %slice_add_fusion, bf16[1,512,128]{2,1,0:T(8,128)(2,1)S(1)} %collective-permute-done.23), kind=kLoop, calls=%fused_computation.6 | loop fusion | flops 262144 | bytes 917504 | tf_op jit(solution)/shard_map/mul | solution.py:251
  (27 shorter events, 0.3 us)
Async XLA Ops:
  0.0 8.1 %collective-permute-start.3 = (bf16[256,256]{1,0:T(8,128)(2,1)}, bf16[256,256]{1,0:T(8,128)(2,1)S(1)}, u32[]{:S(2)}, u32[]{:S(2)}) collective-permute-start(bf16[256,256]{1,0:T(8,128)(2,1)} %bitcast.1), channel_id=1, source_target_pairs={{0,17},{1,16},{2,19},{3,18},{4,21},{5,20},{6,23},{7,22},{8,25},{9,... | collective-permute-start | bytes 393224 | tf_op jit(solution)/shard_map/ppermute | solution.py:21
  3.9 6.5 %collective-permute-start.2 = (bf16[256,256]{1,0:T(8,128)(2,1)}, bf16[256,256]{1,0:T(8,128)(2,1)S(1)}, u32[]{:S(2)}, u32[]{:S(2)}) collective-permute-start(bf16[256,256]{1,0:T(8,128)(2,1)} %bitcast.2), channel_id=1, source_target_pairs={{0,1},{1,0},{2,3},{3,2},{4,5},{5,4},{6,7},{7,6},{8,9},{9,8},{10,11... | collective-permute-start | bytes 393224 | tf_op jit(solution)/shard_map/ppermute | solution.py:21
  4.4 6.3 %collective-permute-start.1 = (bf16[256,256]{1,0:T(8,128)(2,1)}, bf16[256,256]{1,0:T(8,128)(2,1)S(1)}, u32[]{:S(2)}, u32[]{:S(2)}) collective-permute-start(bf16[256,256]{1,0:T(8,128)(2,1)} %bitcast.3), channel_id=1, source_target_pairs={{0,16},{1,17},{2,18},{3,19},{4,20},{5,21},{6,22},{7,23},{8,24},{9,... | collective-permute-start | bytes 393224 | tf_op jit(solution)/shard_map/ppermute | solution.py:21
  4.5 8.8 %collective-permute-start = (bf16[256,256]{1,0:T(8,128)(2,1)}, bf16[256,256]{1,0:T(8,128)(2,1)S(1)}, u32[]{:S(2)}, u32[]{:S(2)}) collective-permute-start(bf16[256,256]{1,0:T(8,128)(2,1)} %bitcast.4), channel_id=1, source_target_pairs={{0,4},{1,5},{2,6},{3,7},{4,0},{5,1},{6,2},{7,3},{8,12},{9,13},{10,... | collective-permute-start | bytes 393224 | tf_op jit(solution)/shard_map/ppermute | solution.py:21
  14.2 9.2 %collective-permute-start.4 = (bf16[512,256]{1,0:T(8,128)(2,1)S(1)}, bf16[512,256]{1,0:T(8,128)(2,1)S(1)}, u32[]{:S(2)}, u32[]{:S(2)}) collective-permute-start(bf16[512,256]{1,0:T(8,128)(2,1)S(1)} %pad_maximum_fusion.1.refs_0_), channel_id=1, source_target_pairs={{0,2},{1,3},{2,0},{3,1},{4,6},{5,7},{6,4},{7,5},{8,10},{9,11},{10,... | collective-permute-start | bytes 786440 | tf_op jit(solution)/shard_map/ppermute | solution.py:21
  15.0 6.8 %collective-permute-start.7 = (bf16[256,256]{1,0:T(8,128)(2,1)S(1)}, bf16[256,256]{1,0:T(8,128)(2,1)S(1)}, u32[]{:S(2)}, u32[]{:S(2)}) collective-permute-start(bf16[256,256]{1,0:T(8,128)(2,1)S(1)} %collective-permute-done), channel_id=1, source_target_pairs={{0,17},{1,16},{2,19},{3,18},{4,21},{5,20},{6,23},{7,22},{8,25},{9,... | collective-permute-start | bytes 393224 | tf_op jit(solution)/shard_map/ppermute | solution.py:21
  17.5 5.8 %collective-permute-start.6 = (bf16[256,256]{1,0:T(8,128)(2,1)S(1)}, bf16[256,256]{1,0:T(8,128)(2,1)S(1)}, u32[]{:S(2)}, u32[]{:S(2)}) collective-permute-start(bf16[256,256]{1,0:T(8,128)(2,1)S(1)} %collective-permute-done), channel_id=1, source_target_pairs={{0,1},{1,0},{2,3},{3,2},{4,5},{5,4},{6,7},{7,6},{8,9},{9,8},{10,11... | collective-permute-start | bytes 393224 | tf_op jit(solution)/shard_map/ppermute | solution.py:21
  18.0 5.3 %collective-permute-start.5 = (bf16[256,256]{1,0:T(8,128)(2,1)S(1)}, bf16[256,256]{1,0:T(8,128)(2,1)S(1)}, u32[]{:S(2)}, u32[]{:S(2)}) collective-permute-start(bf16[256,256]{1,0:T(8,128)(2,1)S(1)} %collective-permute-done), channel_id=1, source_target_pairs={{0,16},{1,17},{2,18},{3,19},{4,20},{5,21},{6,22},{7,23},{8,24},{9,... | collective-permute-start | bytes 393224 | tf_op jit(solution)/shard_map/ppermute | solution.py:21
  18.5 13.8 %collective-permute-start.11 = (bf16[512,256]{1,0:T(8,128)(2,1)S(1)}, bf16[512,256]{1,0:T(8,128)(2,1)S(1)}, u32[]{:S(2)}, u32[]{:S(2)}) collective-permute-start(bf16[512,256]{1,0:T(8,128)(2,1)S(1)} %pad_maximum_fusion.1.refs_0_), channel_id=1, source_target_pairs={{0,8},{1,9},{2,10},{3,11},{4,12},{5,13},{6,14},{7,15},{8,0},{9,1},... | collective-permute-start | bytes 786440 | tf_op jit(solution)/shard_map/ppermute | solution.py:21
  23.3 7.3 %collective-permute-start.10 = (bf16[512,256]{1,0:T(8,128)(2,1)S(1)}, bf16[512,256]{1,0:T(8,128)(2,1)S(1)}, u32[]{:S(2)}, u32[]{:S(2)}) collective-permute-start(bf16[512,256]{1,0:T(8,128)(2,1)S(1)} %constant_dynamic-update-slice_fusion.4.refs_3_), channel_id=1, source_target_pairs={{0,2},{1,3},{2,0},{3,1},{4,6},{5,7},{6,4},{7,5},{8,10},{9,11},{10,... | collective-permute-start | bytes 786440 | tf_op jit(solution)/shard_map/ppermute | solution.py:21
  24.4 6.4 %collective-permute-start.9 = (bf16[512,256]{1,0:T(8,128)(2,1)S(1)}, bf16[512,256]{1,0:T(8,128)(2,1)S(1)}, u32[]{:S(2)}, u32[]{:S(2)}) collective-permute-start(bf16[512,256]{1,0:T(8,128)(2,1)S(1)} %collective-permute-done.4.refs_4_), channel_id=1, source_target_pairs={{0,1},{1,0},{2,3},{3,2},{4,5},{5,4},{6,7},{7,6},{8,9},{9,8},{10,11... | collective-permute-start | bytes 786440 | tf_op jit(solution)/shard_map/ppermute | solution.py:21
  25.9 6.4 %collective-permute-start.8 = (bf16[512,256]{1,0:T(8,128)(2,1)S(1)}, bf16[512,256]{1,0:T(8,128)(2,1)S(1)}, u32[]{:S(2)}, u32[]{:S(2)}) collective-permute-start(bf16[512,256]{1,0:T(8,128)(2,1)S(1)} %collective-permute-done.4.refs_4_), channel_id=1, source_target_pairs={{0,16},{1,17},{2,18},{3,19},{4,20},{5,21},{6,22},{7,23},{8,24},{9,... | collective-permute-start | bytes 786440 | tf_op jit(solution)/shard_map/ppermute | solution.py:21
  26.4 6.3 %collective-permute-start.13 = (bf16[512,256]{1,0:T(8,128)(2,1)S(1)}, bf16[512,256]{1,0:T(8,128)(2,1)S(1)}, u32[]{:S(2)}, u32[]{:S(2)}) collective-permute-start(bf16[512,256]{1,0:T(8,128)(2,1)S(1)} %constant_dynamic-update-slice_fusion.2.refs_2_), channel_id=1, source_target_pairs={{0,8},{1,9},{2,10},{3,11},{4,12},{5,13},{6,14},{7,15},{8,0},{9,1},... | collective-permute-start | bytes 786440 | tf_op jit(solution)/shard_map/ppermute | solution.py:21
  26.5 24.6 %copy-start.2 = (s32[1,2,64]{2,1,0:T(2,128)S(1)}, s32[1,2,64]{2,1,0:T(2,128)}, u32[]{:S(2)}) copy-start(s32[1,2,64]{2,1,0:T(2,128)} %ex_hbm.3) | copy-start | bytes 1540
  30.6 2.3 %collective-permute-start.12 = (bf16[512,256]{1,0:T(8,128)(2,1)S(1)}, bf16[512,256]{1,0:T(8,128)(2,1)S(1)}, u32[]{:S(2)}, u32[]{:S(2)}) collective-permute-start(bf16[512,256]{1,0:T(8,128)(2,1)S(1)} %constant_dynamic-update-slice_fusion.refs_1_), channel_id=1, source_target_pairs={{0,8},{1,9},{2,10},{3,11},{4,12},{5,13},{6,14},{7,15},{8,0},{9,1},... | collective-permute-start | bytes 786440 | tf_op jit(solution)/shard_map/ppermute | solution.py:21
  30.9 2.4 %collective-permute-start.14 = (bf16[512,256]{1,0:T(8,128)(2,1)S(1)}, bf16[512,256]{1,0:T(8,128)(2,1)S(1)}, u32[]{:S(2)}, u32[]{:S(2)}) collective-permute-start(bf16[512,256]{1,0:T(8,128)(2,1)S(1)} %constant_dynamic-update-slice_fusion.4.refs_3_), channel_id=1, source_target_pairs={{0,8},{1,9},{2,10},{3,11},{4,12},{5,13},{6,14},{7,15},{8,0},{9,1},... | collective-permute-start | bytes 786440 | tf_op jit(solution)/shard_map/ppermute | solution.py:21
  32.3 1.5 %collective-permute-start.15 = (bf16[512,256]{1,0:T(8,128)(2,1)S(1)}, bf16[512,256]{1,0:T(8,128)(2,1)S(1)}, u32[]{:S(2)}, u32[]{:S(2)}) collective-permute-start(bf16[512,256]{1,0:T(8,128)(2,1)S(1)} %collective-permute-done.4.refs_4_), channel_id=1, source_target_pairs={{0,8},{1,9},{2,10},{3,11},{4,12},{5,13},{6,14},{7,15},{8,0},{9,1},... | collective-permute-start | bytes 786440 | tf_op jit(solution)/shard_map/ppermute | solution.py:21
  32.3 1.9 %collective-permute-start.16 = (bf16[512,256]{1,0:T(8,128)(2,1)S(1)}, bf16[512,256]{1,0:T(8,128)(2,1)S(1)}, u32[]{:S(2)}, u32[]{:S(2)}) collective-permute-start(bf16[512,256]{1,0:T(8,128)(2,1)S(1)} %collective-permute-done.8.refs_5_), channel_id=1, source_target_pairs={{0,8},{1,9},{2,10},{3,11},{4,12},{5,13},{6,14},{7,15},{8,0},{9,1},... | collective-permute-start | bytes 786440 | tf_op jit(solution)/shard_map/ppermute | solution.py:21
  32.8 1.8 %collective-permute-start.17 = (bf16[512,256]{1,0:T(8,128)(2,1)S(1)}, bf16[512,256]{1,0:T(8,128)(2,1)S(1)}, u32[]{:S(2)}, u32[]{:S(2)}) collective-permute-start(bf16[512,256]{1,0:T(8,128)(2,1)S(1)} %collective-permute-done.9.refs_6_), channel_id=1, source_target_pairs={{0,8},{1,9},{2,10},{3,11},{4,12},{5,13},{6,14},{7,15},{8,0},{9,1},... | collective-permute-start | bytes 786440 | tf_op jit(solution)/shard_map/ppermute | solution.py:21
  32.9 2.1 %collective-permute-start.18 = (bf16[512,256]{1,0:T(8,128)(2,1)S(1)}, bf16[512,256]{1,0:T(8,128)(2,1)S(1)}, u32[]{:S(2)}, u32[]{:S(2)}) collective-permute-start(bf16[512,256]{1,0:T(8,128)(2,1)S(1)} %collective-permute-done.10.refs_7_), channel_id=1, source_target_pairs={{0,8},{1,9},{2,10},{3,11},{4,12},{5,13},{6,14},{7,15},{8,0},{9,1},... | collective-permute-start | bytes 786440 | tf_op jit(solution)/shard_map/ppermute | solution.py:21
  34.9 1.7 %copy-start = (bf16[3,1,1,48,64,128]{5,4,3,2,1,0:T(8,128)(2,1)S(1)}, bf16[3,1,1,48,64,128]{5,4,3,2,1,0:T(8,128)(2,1)}, u32[]{:S(2)}) copy-start(bf16[3,1,1,48,64,128]{5,4,3,2,1,0:T(8,128)(2,1)} %lmat_ref.1) | copy-start | bytes 7077892
  36.6 0.7 copy-start.1
  37.3 0.7 copy-start.3
  38.0 0.7 copy-start.4
  48.8 8.4 %collective-permute-start.19 = (bf16[4,256,128]{2,1,0:T(8,128)(2,1)S(1)}, bf16[4,256,128]{2,1,0:T(8,128)(2,1)S(1)}, u32[]{:S(2)}, u32[]{:S(2)}) collective-permute-start(bf16[4,256,128]{2,1,0:T(8,128)(2,1)S(1)} %get-tuple-element.36), channel_id=1, source_target_pairs={{0,1},{1,0},{2,3},{3,2},{4,5},{5,4},{6,7},{7,6},{8,9},{9,8},{10,11... | collective-permute-start | bytes 786440 | tf_op jit(solution)/shard_map/ppermute | solution.py:21
  49.7 9.3 %collective-permute-start.21 = (bf16[4,256,128]{2,1,0:T(8,128)(2,1)S(1)}, bf16[4,256,128]{2,1,0:T(8,128)(2,1)S(1)}, u32[]{:S(2)}, u32[]{:S(2)}) collective-permute-start(bf16[4,256,128]{2,1,0:T(8,128)(2,1)S(1)} %get-tuple-element.38), channel_id=1, source_target_pairs={{0,2},{1,3},{2,0},{3,1},{4,6},{5,7},{6,4},{7,5},{8,10},{9,11},{10,... | collective-permute-start | bytes 786440 | tf_op jit(solution)/shard_map/ppermute | solution.py:21
  57.3 5.0 %collective-permute-start.20 = (bf16[2,256,128]{2,1,0:T(8,128)(2,1)S(1)}, bf16[2,256,128]{2,1,0:T(8,128)(2,1)S(1)}, u32[]{:S(2)}, u32[]{:S(2)}) collective-permute-start(bf16[2,256,128]{2,1,0:T(8,128)(2,1)S(1)} %slice.48), channel_id=1, source_target_pairs={{0,2},{1,3},{2,0},{3,1},{4,6},{5,7},{6,4},{7,5},{8,10},{9,11},{10,... | collective-permute-start | bytes 393224 | tf_op jit(solution)/shard_map/ppermute | solution.py:21
  59.1 5.0 %collective-permute-start.22 = (bf16[2,256,128]{2,1,0:T(8,128)(2,1)S(1)}, bf16[2,256,128]{2,1,0:T(8,128)(2,1)S(1)}, u32[]{:S(2)}, u32[]{:S(2)}) collective-permute-start(bf16[2,256,128]{2,1,0:T(8,128)(2,1)S(1)} %slice.47), channel_id=1, source_target_pairs={{0,1},{1,0},{2,3},{3,2},{4,5},{5,4},{6,7},{7,6},{8,9},{9,8},{10,11... | collective-permute-start | bytes 393224 | tf_op jit(solution)/shard_map/ppermute | solution.py:21
  64.2 8.0 %collective-permute-start.23 = (bf16[1,512,128]{2,1,0:T(8,128)(2,1)S(1)}, bf16[1,512,128]{2,1,0:T(8,128)(2,1)S(1)}, u32[]{:S(2)}, u32[]{:S(2)}) collective-permute-start(bf16[1,512,128]{2,1,0:T(8,128)(2,1)S(1)} %fusion.3), channel_id=1, source_target_pairs={{0,4},{1,5},{2,6},{3,7},{4,0},{5,1},{6,2},{7,3},{8,12},{9,13},{10,... | collective-permute-start | bytes 393224 | tf_op jit(solution)/shard_map/ppermute | solution.py:21

commit v2 on v1

--- a/solution.py
+++ b/solution.py
@@ -74,11 +74,11 @@
     return [off for off, _ in held], [arr for _, arr in held]
 
 
-def exchange_units(owner_of, second, unit, edge, x_ref, turned_ref, ex_ref, out_ref):
+def exchange_units(owner_of, unit, edge, x_ref, turned_ref, ex_ref, out_ref):
     count, rows, _ = out_ref.shape
     for slot in range(count):
         for step in range(rows // unit):
-            row = owner_of(slot) * (2 * rows) + second * rows + step * unit
+            row = owner_of(slot) * rows + step * unit
             e = row // edge
             lb, rb = ex_ref[0, 0, e], ex_ref[0, 1, e]
             lo = pl.multiple_of(lax.rem(row, edge), unit)
@@ -98,8 +98,8 @@
     offsets, far, orders, nq, nblk, edge, occ, nbl, rows, match_hbm, lists_hbm, ex_hbm, lmat_ref, *refs
 ):
     held = refs[: len(offsets)]
-    first_ref, second_ref, x_ref, turned_ref = refs[len(offsets) : len(offsets) + 4]
-    match_ref, lists_ref, ex_ref, l_ref, ops_ref, sums_ref, sems, small = refs[len(offsets) + 4 :]
+    outs, refs = refs[len(offsets) :][: len(orders)], refs[len(offsets) + len(orders) :]
+    x_ref, turned_ref, match_ref, lists_ref, ex_ref, l_ref, ops_ref, sums_ref, sems, small = refs
     ka, fit = lax.axis_index("ka"), lax.axis_index("fit")
     sub = min(rows, edge)
     loads = [
@@ -155,7 +155,7 @@
             )
             return c
 
-        lax.fori_loop(0, nblk, one_block, 0, unroll=16)
+        lax.fori_loop(0, nblk, one_block, 0, unroll=True)
 
         def one_row(rb, c):
             x = sums_ref[pl.ds(pl.multiple_of(rb * edge, edge), edge), :].astype(jnp.bfloat16)
@@ -164,20 +164,21 @@
             turned_ref[rb, qq * 2 * occ : (qq + 1) * 2 * occ, :] = jnp.concatenate([x, low], axis=0).T
             return c
 
-        lax.fori_loop(0, nbl, one_row, 0, unroll=4)
-
-    unit = min(edge, first_ref.shape[1])
-    for second, ref in enumerate((first_ref, second_ref)):
-        exchange_units(chunk_owner(orders[second]), second, unit, edge, x_ref, turned_ref, ex_ref, ref)
-
-
-def rest_kernel(orders, edge, ex_hbm, x_ref, turned_ref, first_ref, second_ref, ex_ref, sem):
+        lax.fori_loop(0, nbl, one_row, 0, unroll=True)
+
+    unit = min(edge, outs[0].shape[1])
+    for order, ref in zip(orders, outs):
+        exchange_units(chunk_owner(order), unit, edge, x_ref, turned_ref, ex_ref, ref)
+
+
+def rest_kernel(orders, edge, ex_hbm, x_ref, turned_ref, *refs):
+    outs, (ex_ref, sem) = refs[: len(orders)], refs[len(orders) :]
     copy = pltpu.make_async_copy(ex_hbm, ex_ref, sem)
     copy.start()
     copy.wait()
-    unit = min(edge, first_ref.shape[1])
-    for second, ref in enumerate((first_ref, second_ref)):
-        exchange_units(chunk_owner(orders[second]), second, unit, edge, x_ref, turned_ref, ex_ref, ref)
+    unit = min(edge, outs[0].shape[1])
+    for order, ref in zip(orders, outs):
+        exchange_units(chunk_owner(order), unit, edge, x_ref, turned_ref, ex_ref, ref)
 
 
 def on_device(nka, nfit, integrals, block_lists, coeff, match, ex_blocks):
@@ -186,6 +187,11 @@
     nexch = ex_blocks.shape[2]
     nbl = nfit * rows // edge
     offsets, held = gather_shards(coeff, nka, nfit)
+
+    def in_hbm(arr):
+        return pltpu.with_memory_space_constraint(arr, pltpu.HBM)
+
+    tables = [in_hbm(arr) for arr in (match, block_lists, ex_blocks)]
     vmem = pl.BlockSpec(memory_space=pltpu.VMEM)
     hbm = pl.BlockSpec(memory_space=pltpu.HBM)
     params = pltpu.CompilerParams(vmem_limit_bytes=28 * 1024 * 1024)
@@ -193,22 +199,28 @@
 
     bits, far = bits_of(nfit), far_offsets(nfit)
     y, w = bits[:2]
-    keep_a = far + [o ^ w for o in far]
-    keep_b = far + [o ^ y for o in far]
-    send_a = [o ^ y for o in keep_a]
-    send_b = [o ^ w for o in keep_b]
-    count, half = nfit // 2, nexch * edge // nfit // 2
-    out_a, out_b, xmat, turned = pl.pallas_call(
+    near = (y, w, y | w)
+    far_sends = [[o ^ n for o in far[1:]] for n in near]
+    near_sends = [[n] for n in near]
+    chunk = nexch * edge // nfit
+
+    def chunks(orders, dtypes):
+        return [
+            jax.ShapeDtypeStruct((len(order), chunk, 2 * edge), dtype)
+            for order, dtype in zip(orders, dtypes)
+        ]
+
+    *far_out, xmat, turned = pl.pallas_call(
         functools.partial(
-            half_kernel, offsets, far, (send_a, send_b), nq, nblk, edge, occ, nbl, rows
+            half_kernel, offsets, far, far_sends, nq, nblk, edge, occ, nbl, rows
         ),
-        out_shape=[jax.ShapeDtypeStruct((count, half, 2 * edge), bf16)] * 2
+        out_shape=chunks(far_sends, [bf16] * 3)
         + [
             jax.ShapeDtypeStruct((nbl, edge, nq * 2 * occ), bf16),
             jax.ShapeDtypeStruct((nbl, nq * 2 * occ, 2 * edge), bf16),
         ],
         in_specs=[hbm] * 4 + [vmem] * len(held),
-        out_specs=[vmem] * 4,
+        out_specs=[vmem] * 5,
         scratch_shapes=[
             pltpu.SMEM(match.shape, i32),
             pltpu.SMEM(block_lists.shape, i32),
@@ -220,35 +232,39 @@
             pltpu.SemaphoreType.DMA((3,)),
         ],
         compiler_params=params,
-    )(match, block_lists, ex_blocks, integrals, *held)
-    own_a, own_b = pl.pallas_call(
-        functools.partial(rest_kernel, (keep_a, keep_b), edge),
-        out_shape=[jax.ShapeDtypeStruct((count, half, 2 * edge), f32)] * 2,
-        in_specs=[hbm, vmem, vmem],
-        out_specs=[vmem] * 2,
-        scratch_shapes=[pltpu.SMEM(ex_blocks.shape, i32), pltpu.SemaphoreType.DMA],
-        compiler_params=params,
-        cost_estimate=pl.CostEstimate(
-            flops=nexch * edge * edge * 2 * nq * 2 * occ, bytes_accessed=1 << 23, transcendentals=0
-        ),
-    )(ex_blocks, xmat, turned)
+    )(*tables, in_hbm(integrals), *held)
+
+    def rest(orders, dtypes):
+        return pl.pallas_call(
+            functools.partial(rest_kernel, orders, edge),
+            out_shape=chunks(orders, dtypes),
+            in_specs=[hbm, vmem, vmem],
+            out_specs=[vmem] * len(orders),
+            scratch_shapes=[pltpu.SMEM(ex_blocks.shape, i32), pltpu.SemaphoreType.DMA],
+            compiler_params=params,
+            cost_estimate=pl.CostEstimate(
+                flops=nexch * edge * edge * 2 * nq * 2 * occ, bytes_accessed=1 << 23, transcendentals=0
+            ),
+        )(tables[2], xmat, turned)
 
     def swap(arr, dfit):
         return swap_by(arr, nka, nfit, 0, dfit)
 
-    n = count // 2
-    sum_a = own_a + swap(out_a, y).astype(f32)
-    sum_b = own_b + swap(out_b, w).astype(f32)
-    got_a = swap(sum_a[n:].astype(bf16), w)
-    got_b = swap(sum_b[n:].astype(bf16), y)
-    total = jnp.concatenate(
-        [sum_a[:n] + got_a.astype(f32), sum_b[:n] + got_b.astype(f32)], axis=1
-    )
+    *near_out, own = rest(near_sends + [far], [bf16] * 3 + [f32])
+    far_got = [swap(arr, n).astype(f32) for arr, n in zip(far_out, near)]
+    near_got = [swap(arr, n).astype(f32) for arr, n in zip(near_out, near)]
+    parts = own[1:] + far_got[0] + far_got[1] + far_got[2]
+    home = own[:1]
+    size = len(far)
     for bit in bits[:1:-1]:
-        n = n // 2
-        total = total[:n] + swap(total[n:].astype(bf16), bit).astype(f32)
+        size = size // 2
+        came = swap(parts[size - 1 :].astype(bf16), bit).astype(f32)
+        home = home + came[:1]
+        if size > 1:
+            parts = parts[: size - 1] + came[1:]
+    home = home + near_got[0] + near_got[1] + near_got[2]
     factor = -((nq * nfit * occ) ** (-0.5))
-    return total * factor
+    return home * factor
 
 
 def solution(mesh):

time: 73.1 us -> 63.5 us (0.87)
  waiting for transfers between devices: 29.6 us -> 22 us
  local copies, waits for them, and re-layouts: 3.81 us -> 0.06 us
  starting transfers between devices: 24.5 us -> 27 us
  Pallas kernels: 13 us -> 12.2 us
    ppermute x24 -> x26, waiting for transfers between devices: 29.6 us -> 22 us  [swap_by(): return lax.ppermute(arr, AXES, perm)]
    unnamed x13 -> x3, local copies, waits for them, and re-layouts: 3.74 us -> 0.03 us
    ppermute x24 -> x26, starting transfers between devices: 24.5 us -> 27 us  [swap_by(): return lax.ppermute(arr, AXES, perm)]
    pallas_call x2, Pallas kernels: 13 us -> 12.2 us  [the longest x1 8.66 us: on_device(): pl.pallas_call(functools.partial(half_kernel, offsets, far, far_sends, nq...]
  transfers between devices with their start and end apart: 24 -> 26, of which waited for: 18 -> 16; matrix products, arithmetic and copies ran while one was open for 0% -> 0% of each run, Pallas kernels for 4% -> 6%
where the time goes in v2:
time: 63.5 us; the launch traced here: 63.2 us
  starting transfers between devices  27 us (43%)
  waiting for transfers between devices  22 us (35%)
  Pallas kernels  12.2 us (19%)
  other arithmetic  1.77 us (3%)
    ppermute x26, starting transfers between devices, swap_by(): return lax.ppermute(arr, AXES, perm)  27 us
    ppermute x26, waiting for transfers between devices, swap_by(): return lax.ppermute(arr, AXES, perm)  22 us
    pallas_call x1, Pallas kernels, on_device(): pl.pallas_call(functools.partial(half_kernel, offsets, far, far_sends, nq...  8.66 us
    pallas_call x1, Pallas kernels, rest(): pl.pallas_call(functools.partial(rest_kernel, orders, edge), out_shape=ch...  3.56 us
  transfers between devices with their start and end apart: 26, of which 16 were waited for; matrix products, arithmetic and copies ran while one was open for 0% of the time, Pallas kernels for 6%

profile of v2, /device:TPU:0, one launch (start us, length us, event | category | flops | bytes accessed | tf_op | source)
XLA Modules:
  0.0 63.2 jit_solution(11560158713668386134)
XLA Ops:
  0.0 3.9 %collective-permute-start.3 = (bf16[256,256]{1,0:T(8,128)(2,1)}, bf16[256,256]{1,0:T(8,128)(2,1)S(1)}, u32[]{:S(2)}, u32[]{:S(2)}) collective-permute-start(bf16[256,256]{1,0:T(8,128)(2,1)} %bitcast.1), channel_id=1, source_target_pairs={{0,17},{1,16},{2,19},{3,18},{4,21},{5,20},{6,23},{7,22},{8,25},{9,... | collective-permute-start | bytes 393224 | tf_op jit(solution)/shard_map/ppermute | solution.py:21
  3.9 0.5 collective-permute-start.2
  4.4 0.1 collective-permute-start.1
  4.5 3.1 %collective-permute-start = (bf16[256,256]{1,0:T(8,128)(2,1)}, bf16[256,256]{1,0:T(8,128)(2,1)S(1)}, u32[]{:S(2)}, u32[]{:S(2)}) collective-permute-start(bf16[256,256]{1,0:T(8,128)(2,1)} %bitcast.4), channel_id=1, source_target_pairs={{0,4},{1,5},{2,6},{3,7},{4,0},{5,1},{6,2},{7,3},{8,12},{9,13},{10,... | collective-permute-start | bytes 393224 | tf_op jit(solution)/shard_map/ppermute | solution.py:21
  7.5 0.6 collective-permute-done.3
  8.1 2.3 %collective-permute-done.2 = bf16[256,256]{1,0:T(8,128)(2,1)S(1)} collective-permute-done((bf16[256,256]{1,0:T(8,128)(2,1)}, bf16[256,256]{1,0:T(8,128)(2,1)S(1)}, u32[]{:S(2)}, u32[]{:S(2)}) %collective-permute-start.2) | collective-permute-done | bytes 131104 | tf_op jit(solution)/shard_map/ppermute | solution.py:21
  10.4 0.3 collective-permute-done.1
  10.7 2.6 %collective-permute-done = bf16[256,256]{1,0:T(8,128)(2,1)S(1)} collective-permute-done((bf16[256,256]{1,0:T(8,128)(2,1)}, bf16[256,256]{1,0:T(8,128)(2,1)S(1)}, u32[]{:S(2)}, u32[]{:S(2)}) %collective-permute-start) | collective-permute-done | bytes 131104 | tf_op jit(solution)/shard_map/ppermute | solution.py:21
  13.2 0.9 %pad_maximum_fusion.refs_0_ = bf16[512,256]{1,0:T(8,128)(2,1)S(1)} fusion(bf16[256,256]{1,0:T(8,128)(2,1)S(1)} %collective-permute-done, bf16[256,256]{1,0:T(8,128)(2,1)} %bitcast.5), kind=kLoop, calls=%fused_computation | loop fusion | flops 524288 | bytes 524288 | tf_op jit(solution)/shard_map/concatenate | solution.py:40
  14.2 0.9 %collective-permute-start.4 = (bf16[512,256]{1,0:T(8,128)(2,1)S(1)}, bf16[512,256]{1,0:T(8,128)(2,1)S(1)}, u32[]{:S(2)}, u32[]{:S(2)}) collective-permute-start(bf16[512,256]{1,0:T(8,128)(2,1)S(1)} %pad_maximum_fusion.refs_0_), channel_id=1, source_target_pairs={{0,2},{1,3},{2,0},{3,1},{4,6},{5,7},{6,4},{7,5},{8,10},{9,11},{10,... | collective-permute-start | bytes 786440 | tf_op jit(solution)/shard_map/ppermute | solution.py:21
  15.0 2.4 %collective-permute-start.7 = (bf16[256,256]{1,0:T(8,128)(2,1)S(1)}, bf16[256,256]{1,0:T(8,128)(2,1)S(1)}, u32[]{:S(2)}, u32[]{:S(2)}) collective-permute-start(bf16[256,256]{1,0:T(8,128)(2,1)S(1)} %collective-permute-done), channel_id=1, source_target_pairs={{0,17},{1,16},{2,19},{3,18},{4,21},{5,20},{6,23},{7,22},{8,25},{9,... | collective-permute-start | bytes 393224 | tf_op jit(solution)/shard_map/ppermute | solution.py:21
  17.5 0.5 collective-permute-start.6
  18.0 0.5 collective-permute-start.5
  18.5 0.0 collective-permute-start.11
  18.5 3.2 %collective-permute-done.7 = bf16[256,256]{1,0:T(8,128)(2,1)S(1)} collective-permute-done((bf16[256,256]{1,0:T(8,128)(2,1)S(1)}, bf16[256,256]{1,0:T(8,128)(2,1)S(1)}, u32[]{:S(2)}, u32[]{:S(2)}) %collective-permute-start.7) | collective-permute-done | bytes 131104 | tf_op jit(solution)/shard_map/ppermute | solution.py:21
  21.8 1.5 %collective-permute-done.6 = bf16[256,256]{1,0:T(8,128)(2,1)S(1)} collective-permute-done((bf16[256,256]{1,0:T(8,128)(2,1)S(1)}, bf16[256,256]{1,0:T(8,128)(2,1)S(1)}, u32[]{:S(2)}, u32[]{:S(2)}) %collective-permute-start.6) | collective-permute-done | bytes 131104 | tf_op jit(solution)/shard_map/ppermute | solution.py:21
  23.2 0.1 collective-permute-done.5
  23.3 0.0 collective-permute-done.4.refs_4_
  23.3 1.1 %collective-permute-start.10 = (bf16[512,256]{1,0:T(8,128)(2,1)S(1)}, bf16[512,256]{1,0:T(8,128)(2,1)S(1)}, u32[]{:S(2)}, u32[]{:S(2)}) collective-permute-start(bf16[512,256]{1,0:T(8,128)(2,1)S(1)} %constant_dynamic-update-slice_fusion.4.refs_3_), channel_id=1, source_target_pairs={{0,2},{1,3},{2,0},{3,1},{4,6},{5,7},{6,4},{7,5},{8,10},{9,11},{10,... | collective-permute-start | bytes 786440 | tf_op jit(solution)/shard_map/ppermute | solution.py:21
  24.4 1.5 %collective-permute-start.9 = (bf16[512,256]{1,0:T(8,128)(2,1)S(1)}, bf16[512,256]{1,0:T(8,128)(2,1)S(1)}, u32[]{:S(2)}, u32[]{:S(2)}) collective-permute-start(bf16[512,256]{1,0:T(8,128)(2,1)S(1)} %collective-permute-done.4.refs_4_), channel_id=1, source_target_pairs={{0,1},{1,0},{2,3},{3,2},{4,5},{5,4},{6,7},{7,6},{8,9},{9,8},{10,11... | collective-permute-start | bytes 786440 | tf_op jit(solution)/shard_map/ppermute | solution.py:21
  25.9 0.5 collective-permute-start.8
  26.4 0.1 collective-permute-start.13
  26.5 4.0 %collective-permute-done.10.refs_7_ = bf16[512,256]{1,0:T(8,128)(2,1)S(1)} collective-permute-done((bf16[512,256]{1,0:T(8,128)(2,1)S(1)}, bf16[512,256]{1,0:T(8,128)(2,1)S(1)}, u32[]{:S(2)}, u32[]{:S(2)}) %collective-permute-start.10) | collective-permute-done | bytes 262176 | tf_op jit(solution)/shard_map/ppermute | solution.py:21
  30.6 0.0 collective-permute-start.12
  30.6 0.3 collective-permute-done.9.refs_6_
  30.9 0.3 collective-permute-start.14
  31.1 1.2 %collective-permute-done.8.refs_5_ = bf16[512,256]{1,0:T(8,128)(2,1)S(1)} collective-permute-done((bf16[512,256]{1,0:T(8,128)(2,1)S(1)}, bf16[512,256]{1,0:T(8,128)(2,1)S(1)}, u32[]{:S(2)}, u32[]{:S(2)}) %collective-permute-start.8) | collective-permute-done | bytes 262176 | tf_op jit(solution)/shard_map/ppermute | solution.py:21
  32.3 0.5 collective-permute-start.16
  32.8 0.1 collective-permute-start.17
  32.9 0.0 collective-permute-done.12.refs_9_
  32.9 0.4 collective-permute-start.18
  33.3 0.5 collective-permute-done.15.refs_12_
  33.8 0.4 collective-permute-done.16.refs_13_
  34.2 0.4 collective-permute-done.17.refs_14_
  34.5 0.4 collective-permute-done.18.refs_15_
  34.9 8.7 %shard_map.55 = (bf16[1,512,128]{2,1,0:T(8,128)(2,1)S(1)}, bf16[1,512,128]{2,1,0:T(8,128)(2,1)S(1)}, bf16[1,512,128]{2,1,0:T(8,128)(2,1)S(1)}, bf16[16,64,1536]{...) custom-call(s32[3,4]{1,0:T(4,128)} %match_hbm.1, s32[3,1,1,2,48]{4,3,2,1,0:T(2,128)} %lists_hbm.1, s32[1,2,64]{2,1,0:T(2,128)} %ex_hbm.3, ...), custom_call_target="tpu_custom_call" | custom-call | tf_op jit(solution)/shard_map/pallas_call | solution.py:213
  43.6 0.9 %collective-permute-start.19 = (bf16[1,512,128]{2,1,0:T(8,128)(2,1)S(1)}, bf16[1,512,128]{2,1,0:T(8,128)(2,1)S(1)}, u32[]{:S(2)}, u32[]{:S(2)}) collective-permute-start(bf16[1,512,128]{2,1,0:T(8,128)(2,1)S(1)} %get-tuple-element.39), channel_id=1, source_target_pairs={{0,1},{1,0},{2,3},{3,2},{4,5},{5,4},{6,7},{7,6},{8,9},{9,8},{10,11... | collective-permute-start | bytes 393224 | tf_op jit(solution)/shard_map/ppermute | solution.py:21
  44.5 1.4 %collective-permute-start.20 = (bf16[1,512,128]{2,1,0:T(8,128)(2,1)S(1)}, bf16[1,512,128]{2,1,0:T(8,128)(2,1)S(1)}, u32[]{:S(2)}, u32[]{:S(2)}) collective-permute-start(bf16[1,512,128]{2,1,0:T(8,128)(2,1)S(1)} %get-tuple-element.40), channel_id=1, source_target_pairs={{0,2},{1,3},{2,0},{3,1},{4,6},{5,7},{6,4},{7,5},{8,10},{9,11},{10,... | collective-permute-start | bytes 393224 | tf_op jit(solution)/shard_map/ppermute | solution.py:21
  46.0 1.2 %collective-permute-start.21 = (bf16[1,512,128]{2,1,0:T(8,128)(2,1)S(1)}, bf16[1,512,128]{2,1,0:T(8,128)(2,1)S(1)}, u32[]{:S(2)}, u32[]{:S(2)}) collective-permute-start(bf16[1,512,128]{2,1,0:T(8,128)(2,1)S(1)} %get-tuple-element.41), channel_id=1, source_target_pairs={{0,3},{1,2},{2,1},{3,0},{4,7},{5,6},{6,5},{7,4},{8,11},{9,10},{10,... | collective-permute-start | bytes 393224 | tf_op jit(solution)/shard_map/ppermute | solution.py:21
  47.2 3.6 %shard_map.56 = (bf16[1,512,128]{2,1,0:T(8,128)(2,1)S(1)}, bf16[1,512,128]{2,1,0:T(8,128)(2,1)S(1)}, bf16[1,512,128]{2,1,0:T(8,128)(2,1)S(1)}, f32[2,512,128]{2,1,0:T(8,128)S(1)}) custom-call(s32[1,2,64]{2,1,0:T(2,128)} %ex_hbm.3, bf16[16,64,1536]{2,1,0:T(8,128)(2,1)S(1)} %get-tuple-element.36.x_ref, bf16[16,1536,128]{2,1,0:T(8,128)(2,1)S(1)} %get-tuple-element.37.turned_ref), custom_call_target="tpu_custom_call" | custom-call | flops 805306368 | bytes 8388608 | tf_op jit(solution)/shard_map/pallas_call | solution.py:238
  50.7 0.9 %collective-permute-start.23 = (bf16[1,512,128]{2,1,0:T(8,128)(2,1)S(1)}, bf16[1,512,128]{2,1,0:T(8,128)(2,1)S(1)}, u32[]{:S(2)}, u32[]{:S(2)}) collective-permute-start(bf16[1,512,128]{2,1,0:T(8,128)(2,1)S(1)} %get-tuple-element.42), channel_id=1, source_target_pairs={{0,1},{1,0},{2,3},{3,2},{4,5},{5,4},{6,7},{7,6},{8,9},{9,8},{10,11... | collective-permute-start | bytes 393224 | tf_op jit(solution)/shard_map/ppermute | solution.py:21
  51.7 1.4 %collective-permute-start.24 = (bf16[1,512,128]{2,1,0:T(8,128)(2,1)S(1)}, bf16[1,512,128]{2,1,0:T(8,128)(2,1)S(1)}, u32[]{:S(2)}, u32[]{:S(2)}) collective-permute-start(bf16[1,512,128]{2,1,0:T(8,128)(2,1)S(1)} %get-tuple-element.43), channel_id=1, source_target_pairs={{0,2},{1,3},{2,0},{3,1},{4,6},{5,7},{6,4},{7,5},{8,10},{9,11},{10,... | collective-permute-start | bytes 393224 | tf_op jit(solution)/shard_map/ppermute | solution.py:21
  53.1 1.2 %collective-permute-start.25 = (bf16[1,512,128]{2,1,0:T(8,128)(2,1)S(1)}, bf16[1,512,128]{2,1,0:T(8,128)(2,1)S(1)}, u32[]{:S(2)}, u32[]{:S(2)}) collective-permute-start(bf16[1,512,128]{2,1,0:T(8,128)(2,1)S(1)} %get-tuple-element.44), channel_id=1, source_target_pairs={{0,3},{1,2},{2,1},{3,0},{4,7},{5,6},{6,5},{7,4},{8,11},{9,10},{10,... | collective-permute-start | bytes 393224 | tf_op jit(solution)/shard_map/ppermute | solution.py:21
  54.3 0.1 add_convert_fusion
  54.4 3.6 %collective-permute-start.22 = (bf16[1,512,128]{2,1,0:T(8,128)(2,1)S(1)}, bf16[1,512,128]{2,1,0:T(8,128)(2,1)S(1)}, u32[]{:S(2)}, u32[]{:S(2)}) collective-permute-start(bf16[1,512,128]{2,1,0:T(8,128)(2,1)S(1)} %add_convert_fusion), channel_id=1, source_target_pairs={{0,4},{1,5},{2,6},{3,7},{4,0},{5,1},{6,2},{7,3},{8,12},{9,13},{10,... | collective-permute-start | bytes 393224 | tf_op jit(solution)/shard_map/ppermute | solution.py:21
  57.9 1.5 %collective-permute-done.24 = bf16[1,512,128]{2,1,0:T(8,128)(2,1)S(1)} collective-permute-done((bf16[1,512,128]{2,1,0:T(8,128)(2,1)S(1)}, bf16[1,512,128]{2,1,0:T(8,128)(2,1)S(1)}, u32[]{:S(2)}, u32[]{:S(2)}) %collective-permute-start.24) | collective-permute-done | bytes 131104 | tf_op jit(solution)/shard_map/ppermute | solution.py:21
  59.4 3.0 %collective-permute-done.25 = bf16[1,512,128]{2,1,0:T(8,128)(2,1)S(1)} collective-permute-done((bf16[1,512,128]{2,1,0:T(8,128)(2,1)S(1)}, bf16[1,512,128]{2,1,0:T(8,128)(2,1)S(1)}, u32[]{:S(2)}, u32[]{:S(2)}) %collective-permute-start.25) | collective-permute-done | bytes 131104 | tf_op jit(solution)/shard_map/ppermute | solution.py:21
  62.4 0.8 %add_multiply_fusion = f32[1,512,128]{2,1,0:T(8,128)} fusion(bf16[1,512,128]{2,1,0:T(8,128)(2,1)S(1)} %collective-permute-done.25, bf16[1,512,128]{2,1,0:T(8,128)(2,1)S(1)} %collective-permute-done.24, bf16[1,512,128]{2,1,0:T(8,128)(2,1)S(1)} %collective-permute-done.23, bf16[1,512,128]{2,1,0:T(8,128)(2,1)S(1)} %collective-permute-done.22, ...), kind=kLoop, calls=%fused_computation.1 | loop fusion | flops 589824 | bytes 1048576 | tf_op jit(solution)/shard_map/mul | solution.py:267
  (15 shorter events, 0.1 us)
Async XLA Ops:
  0.0 8.1 %collective-permute-start.3 = (bf16[256,256]{1,0:T(8,128)(2,1)}, bf16[256,256]{1,0:T(8,128)(2,1)S(1)}, u32[]{:S(2)}, u32[]{:S(2)}) collective-permute-start(bf16[256,256]{1,0:T(8,128)(2,1)} %bitcast.1), channel_id=1, source_target_pairs={{0,17},{1,16},{2,19},{3,18},{4,21},{5,20},{6,23},{7,22},{8,25},{9,... | collective-permute-start | bytes 393224 | tf_op jit(solution)/shard_map/ppermute | solution.py:21
  3.9 6.5 %collective-permute-start.2 = (bf16[256,256]{1,0:T(8,128)(2,1)}, bf16[256,256]{1,0:T(8,128)(2,1)S(1)}, u32[]{:S(2)}, u32[]{:S(2)}) collective-permute-start(bf16[256,256]{1,0:T(8,128)(2,1)} %bitcast.2), channel_id=1, source_target_pairs={{0,1},{1,0},{2,3},{3,2},{4,5},{5,4},{6,7},{7,6},{8,9},{9,8},{10,11... | collective-permute-start | bytes 393224 | tf_op jit(solution)/shard_map/ppermute | solution.py:21
  4.4 6.3 %collective-permute-start.1 = (bf16[256,256]{1,0:T(8,128)(2,1)}, bf16[256,256]{1,0:T(8,128)(2,1)S(1)}, u32[]{:S(2)}, u32[]{:S(2)}) collective-permute-start(bf16[256,256]{1,0:T(8,128)(2,1)} %bitcast.3), channel_id=1, source_target_pairs={{0,16},{1,17},{2,18},{3,19},{4,20},{5,21},{6,22},{7,23},{8,24},{9,... | collective-permute-start | bytes 393224 | tf_op jit(solution)/shard_map/ppermute | solution.py:21
  4.5 8.8 %collective-permute-start = (bf16[256,256]{1,0:T(8,128)(2,1)}, bf16[256,256]{1,0:T(8,128)(2,1)S(1)}, u32[]{:S(2)}, u32[]{:S(2)}) collective-permute-start(bf16[256,256]{1,0:T(8,128)(2,1)} %bitcast.4), channel_id=1, source_target_pairs={{0,4},{1,5},{2,6},{3,7},{4,0},{5,1},{6,2},{7,3},{8,12},{9,13},{10,... | collective-permute-start | bytes 393224 | tf_op jit(solution)/shard_map/ppermute | solution.py:21
  14.2 9.2 %collective-permute-start.4 = (bf16[512,256]{1,0:T(8,128)(2,1)S(1)}, bf16[512,256]{1,0:T(8,128)(2,1)S(1)}, u32[]{:S(2)}, u32[]{:S(2)}) collective-permute-start(bf16[512,256]{1,0:T(8,128)(2,1)S(1)} %pad_maximum_fusion.refs_0_), channel_id=1, source_target_pairs={{0,2},{1,3},{2,0},{3,1},{4,6},{5,7},{6,4},{7,5},{8,10},{9,11},{10,... | collective-permute-start | bytes 786440 | tf_op jit(solution)/shard_map/ppermute | solution.py:21
  15.0 6.8 %collective-permute-start.7 = (bf16[256,256]{1,0:T(8,128)(2,1)S(1)}, bf16[256,256]{1,0:T(8,128)(2,1)S(1)}, u32[]{:S(2)}, u32[]{:S(2)}) collective-permute-start(bf16[256,256]{1,0:T(8,128)(2,1)S(1)} %collective-permute-done), channel_id=1, source_target_pairs={{0,17},{1,16},{2,19},{3,18},{4,21},{5,20},{6,23},{7,22},{8,25},{9,... | collective-permute-start | bytes 393224 | tf_op jit(solution)/shard_map/ppermute | solution.py:21
  17.5 5.8 %collective-permute-start.6 = (bf16[256,256]{1,0:T(8,128)(2,1)S(1)}, bf16[256,256]{1,0:T(8,128)(2,1)S(1)}, u32[]{:S(2)}, u32[]{:S(2)}) collective-permute-start(bf16[256,256]{1,0:T(8,128)(2,1)S(1)} %collective-permute-done), channel_id=1, source_target_pairs={{0,1},{1,0},{2,3},{3,2},{4,5},{5,4},{6,7},{7,6},{8,9},{9,8},{10,11... | collective-permute-start | bytes 393224 | tf_op jit(solution)/shard_map/ppermute | solution.py:21
  18.0 5.3 %collective-permute-start.5 = (bf16[256,256]{1,0:T(8,128)(2,1)S(1)}, bf16[256,256]{1,0:T(8,128)(2,1)S(1)}, u32[]{:S(2)}, u32[]{:S(2)}) collective-permute-start(bf16[256,256]{1,0:T(8,128)(2,1)S(1)} %collective-permute-done), channel_id=1, source_target_pairs={{0,16},{1,17},{2,18},{3,19},{4,20},{5,21},{6,22},{7,23},{8,24},{9,... | collective-permute-start | bytes 393224 | tf_op jit(solution)/shard_map/ppermute | solution.py:21
  18.5 13.8 %collective-permute-start.11 = (bf16[512,256]{1,0:T(8,128)(2,1)S(1)}, bf16[512,256]{1,0:T(8,128)(2,1)S(1)}, u32[]{:S(2)}, u32[]{:S(2)}) collective-permute-start(bf16[512,256]{1,0:T(8,128)(2,1)S(1)} %pad_maximum_fusion.refs_0_), channel_id=1, source_target_pairs={{0,8},{1,9},{2,10},{3,11},{4,12},{5,13},{6,14},{7,15},{8,0},{9,1},... | collective-permute-start | bytes 786440 | tf_op jit(solution)/shard_map/ppermute | solution.py:21
  23.3 7.3 %collective-permute-start.10 = (bf16[512,256]{1,0:T(8,128)(2,1)S(1)}, bf16[512,256]{1,0:T(8,128)(2,1)S(1)}, u32[]{:S(2)}, u32[]{:S(2)}) collective-permute-start(bf16[512,256]{1,0:T(8,128)(2,1)S(1)} %constant_dynamic-update-slice_fusion.4.refs_3_), channel_id=1, source_target_pairs={{0,2},{1,3},{2,0},{3,1},{4,6},{5,7},{6,4},{7,5},{8,10},{9,11},{10,... | collective-permute-start | bytes 786440 | tf_op jit(solution)/shard_map/ppermute | solution.py:21
  24.4 6.4 %collective-permute-start.9 = (bf16[512,256]{1,0:T(8,128)(2,1)S(1)}, bf16[512,256]{1,0:T(8,128)(2,1)S(1)}, u32[]{:S(2)}, u32[]{:S(2)}) collective-permute-start(bf16[512,256]{1,0:T(8,128)(2,1)S(1)} %collective-permute-done.4.refs_4_), channel_id=1, source_target_pairs={{0,1},{1,0},{2,3},{3,2},{4,5},{5,4},{6,7},{7,6},{8,9},{9,8},{10,11... | collective-permute-start | bytes 786440 | tf_op jit(solution)/shard_map/ppermute | solution.py:21
  25.9 6.4 %collective-permute-start.8 = (bf16[512,256]{1,0:T(8,128)(2,1)S(1)}, bf16[512,256]{1,0:T(8,128)(2,1)S(1)}, u32[]{:S(2)}, u32[]{:S(2)}) collective-permute-start(bf16[512,256]{1,0:T(8,128)(2,1)S(1)} %collective-permute-done.4.refs_4_), channel_id=1, source_target_pairs={{0,16},{1,17},{2,18},{3,19},{4,20},{5,21},{6,22},{7,23},{8,24},{9,... | collective-permute-start | bytes 786440 | tf_op jit(solution)/shard_map/ppermute | solution.py:21
  26.4 6.3 %collective-permute-start.13 = (bf16[512,256]{1,0:T(8,128)(2,1)S(1)}, bf16[512,256]{1,0:T(8,128)(2,1)S(1)}, u32[]{:S(2)}, u32[]{:S(2)}) collective-permute-start(bf16[512,256]{1,0:T(8,128)(2,1)S(1)} %constant_dynamic-update-slice_fusion.2.refs_2_), channel_id=1, source_target_pairs={{0,8},{1,9},{2,10},{3,11},{4,12},{5,13},{6,14},{7,15},{8,0},{9,1},... | collective-permute-start | bytes 786440 | tf_op jit(solution)/shard_map/ppermute | solution.py:21
  30.6 2.3 %collective-permute-start.12 = (bf16[512,256]{1,0:T(8,128)(2,1)S(1)}, bf16[512,256]{1,0:T(8,128)(2,1)S(1)}, u32[]{:S(2)}, u32[]{:S(2)}) collective-permute-start(bf16[512,256]{1,0:T(8,128)(2,1)S(1)} %constant_dynamic-update-slice_fusion.refs_1_), channel_id=1, source_target_pairs={{0,8},{1,9},{2,10},{3,11},{4,12},{5,13},{6,14},{7,15},{8,0},{9,1},... | collective-permute-start | bytes 786440 | tf_op jit(solution)/shard_map/ppermute | solution.py:21
  30.9 2.4 %collective-permute-start.14 = (bf16[512,256]{1,0:T(8,128)(2,1)S(1)}, bf16[512,256]{1,0:T(8,128)(2,1)S(1)}, u32[]{:S(2)}, u32[]{:S(2)}) collective-permute-start(bf16[512,256]{1,0:T(8,128)(2,1)S(1)} %constant_dynamic-update-slice_fusion.4.refs_3_), channel_id=1, source_target_pairs={{0,8},{1,9},{2,10},{3,11},{4,12},{5,13},{6,14},{7,15},{8,0},{9,1},... | collective-permute-start | bytes 786440 | tf_op jit(solution)/shard_map/ppermute | solution.py:21
  32.3 1.5 %collective-permute-start.15 = (bf16[512,256]{1,0:T(8,128)(2,1)S(1)}, bf16[512,256]{1,0:T(8,128)(2,1)S(1)}, u32[]{:S(2)}, u32[]{:S(2)}) collective-permute-start(bf16[512,256]{1,0:T(8,128)(2,1)S(1)} %collective-permute-done.4.refs_4_), channel_id=1, source_target_pairs={{0,8},{1,9},{2,10},{3,11},{4,12},{5,13},{6,14},{7,15},{8,0},{9,1},... | collective-permute-start | bytes 786440 | tf_op jit(solution)/shard_map/ppermute | solution.py:21
  32.3 1.9 %collective-permute-start.16 = (bf16[512,256]{1,0:T(8,128)(2,1)S(1)}, bf16[512,256]{1,0:T(8,128)(2,1)S(1)}, u32[]{:S(2)}, u32[]{:S(2)}) collective-permute-start(bf16[512,256]{1,0:T(8,128)(2,1)S(1)} %collective-permute-done.8.refs_5_), channel_id=1, source_target_pairs={{0,8},{1,9},{2,10},{3,11},{4,12},{5,13},{6,14},{7,15},{8,0},{9,1},... | collective-permute-start | bytes 786440 | tf_op jit(solution)/shard_map/ppermute | solution.py:21
  32.8 1.8 %collective-permute-start.17 = (bf16[512,256]{1,0:T(8,128)(2,1)S(1)}, bf16[512,256]{1,0:T(8,128)(2,1)S(1)}, u32[]{:S(2)}, u32[]{:S(2)}) collective-permute-start(bf16[512,256]{1,0:T(8,128)(2,1)S(1)} %collective-permute-done.9.refs_6_), channel_id=1, source_target_pairs={{0,8},{1,9},{2,10},{3,11},{4,12},{5,13},{6,14},{7,15},{8,0},{9,1},... | collective-permute-start | bytes 786440 | tf_op jit(solution)/shard_map/ppermute | solution.py:21
  32.9 2.1 %collective-permute-start.18 = (bf16[512,256]{1,0:T(8,128)(2,1)S(1)}, bf16[512,256]{1,0:T(8,128)(2,1)S(1)}, u32[]{:S(2)}, u32[]{:S(2)}) collective-permute-start(bf16[512,256]{1,0:T(8,128)(2,1)S(1)} %collective-permute-done.10.refs_7_), channel_id=1, source_target_pairs={{0,8},{1,9},{2,10},{3,11},{4,12},{5,13},{6,14},{7,15},{8,0},{9,1},... | collective-permute-start | bytes 786440 | tf_op jit(solution)/shard_map/ppermute | solution.py:21
  43.6 9.5 %collective-permute-start.19 = (bf16[1,512,128]{2,1,0:T(8,128)(2,1)S(1)}, bf16[1,512,128]{2,1,0:T(8,128)(2,1)S(1)}, u32[]{:S(2)}, u32[]{:S(2)}) collective-permute-start(bf16[1,512,128]{2,1,0:T(8,128)(2,1)S(1)} %get-tuple-element.39), channel_id=1, source_target_pairs={{0,1},{1,0},{2,3},{3,2},{4,5},{5,4},{6,7},{7,6},{8,9},{9,8},{10,11... | collective-permute-start | bytes 393224 | tf_op jit(solution)/shard_map/ppermute | solution.py:21
  44.5 9.7 %collective-permute-start.20 = (bf16[1,512,128]{2,1,0:T(8,128)(2,1)S(1)}, bf16[1,512,128]{2,1,0:T(8,128)(2,1)S(1)}, u32[]{:S(2)}, u32[]{:S(2)}) collective-permute-start(bf16[1,512,128]{2,1,0:T(8,128)(2,1)S(1)} %get-tuple-element.40), channel_id=1, source_target_pairs={{0,2},{1,3},{2,0},{3,1},{4,6},{5,7},{6,4},{7,5},{8,10},{9,11},{10,... | collective-permute-start | bytes 393224 | tf_op jit(solution)/shard_map/ppermute | solution.py:21
  46.0 8.3 %collective-permute-start.21 = (bf16[1,512,128]{2,1,0:T(8,128)(2,1)S(1)}, bf16[1,512,128]{2,1,0:T(8,128)(2,1)S(1)}, u32[]{:S(2)}, u32[]{:S(2)}) collective-permute-start(bf16[1,512,128]{2,1,0:T(8,128)(2,1)S(1)} %get-tuple-element.41), channel_id=1, source_target_pairs={{0,3},{1,2},{2,1},{3,0},{4,7},{5,6},{6,5},{7,4},{8,11},{9,10},{10,... | collective-permute-start | bytes 393224 | tf_op jit(solution)/shard_map/ppermute | solution.py:21
  50.7 7.2 %collective-permute-start.23 = (bf16[1,512,128]{2,1,0:T(8,128)(2,1)S(1)}, bf16[1,512,128]{2,1,0:T(8,128)(2,1)S(1)}, u32[]{:S(2)}, u32[]{:S(2)}) collective-permute-start(bf16[1,512,128]{2,1,0:T(8,128)(2,1)S(1)} %get-tuple-element.42), channel_id=1, source_target_pairs={{0,1},{1,0},{2,3},{3,2},{4,5},{5,4},{6,7},{7,6},{8,9},{9,8},{10,11... | collective-permute-start | bytes 393224 | tf_op jit(solution)/shard_map/ppermute | solution.py:21
  51.7 7.7 %collective-permute-start.24 = (bf16[1,512,128]{2,1,0:T(8,128)(2,1)S(1)}, bf16[1,512,128]{2,1,0:T(8,128)(2,1)S(1)}, u32[]{:S(2)}, u32[]{:S(2)}) collective-permute-start(bf16[1,512,128]{2,1,0:T(8,128)(2,1)S(1)} %get-tuple-element.43), channel_id=1, source_target_pairs={{0,2},{1,3},{2,0},{3,1},{4,6},{5,7},{6,4},{7,5},{8,10},{9,11},{10,... | collective-permute-start | bytes 393224 | tf_op jit(solution)/shard_map/ppermute | solution.py:21
  53.1 9.3 %collective-permute-start.25 = (bf16[1,512,128]{2,1,0:T(8,128)(2,1)S(1)}, bf16[1,512,128]{2,1,0:T(8,128)(2,1)S(1)}, u32[]{:S(2)}, u32[]{:S(2)}) collective-permute-start(bf16[1,512,128]{2,1,0:T(8,128)(2,1)S(1)} %get-tuple-element.44), channel_id=1, source_target_pairs={{0,3},{1,2},{2,1},{3,0},{4,7},{5,6},{6,5},{7,4},{8,11},{9,10},{10,... | collective-permute-start | bytes 393224 | tf_op jit(solution)/shard_map/ppermute | solution.py:21
  54.4 8.0 %collective-permute-start.22 = (bf16[1,512,128]{2,1,0:T(8,128)(2,1)S(1)}, bf16[1,512,128]{2,1,0:T(8,128)(2,1)S(1)}, u32[]{:S(2)}, u32[]{:S(2)}) collective-permute-start(bf16[1,512,128]{2,1,0:T(8,128)(2,1)S(1)} %add_convert_fusion), channel_id=1, source_target_pairs={{0,4},{1,5},{2,6},{3,7},{4,0},{5,1},{6,2},{7,3},{8,12},{9,13},{10,... | collective-permute-start | bytes 393224 | tf_op jit(solution)/shard_map/ppermute | solution.py:21

commit v3 on v2

--- a/solution.py
+++ b/solution.py
@@ -44,15 +44,17 @@
     near = both = own
     for bit in bits[:-1]:
         near = both = join(both, swap(both, 0, bit))
-    far, x_near, y_near, xy_near = lax.optimization_barrier(
+    room = join(near, jnp.zeros_like(near))
+    room, far, x_near, y_near, xy_near = lax.optimization_barrier(
         (
+            room,
             swap(near, 0, bits[-1]),
             swap(near, half, 0),
             swap(near, 0, y),
             swap(near, half, y),
         )
     )
-    both = join(near, far)
+    both = lax.dynamic_update_slice(room, far, (near.shape[0], 0))
     w_both, x_far, y_far, xy_far = lax.optimization_barrier(
         (swap(both, 0, w), swap(far, half, 0), swap(far, 0, y), swap(far, half, y))
     )

time: 63.5 us -> 62.5 us (0.984)
  local copies, waits for them, and re-layouts: 0.06 us -> 1.02 us
  other arithmetic: 1.77 us -> 0.85 us
  waiting for transfers between devices: 22 us -> 21.1 us
    ppermute x26, waiting for transfers between devices: 22 us -> 21.1 us  [swap_by(): return lax.ppermute(arr, AXES, perm)]
    concatenate x3 -> x4, local copies, waits for them, and re-layouts: 0.03 us -> 0.98 us  [join(): return jnp.concatenate(arrs, axis=0)]
    concatenate x1 -> x0, other arithmetic: 0.92 us -> none  [join(): return jnp.concatenate(arrs, axis=0)]
  transfers between devices with their start and end apart: 26 -> 26, of which waited for: 16 -> 15; matrix products, arithmetic and copies ran while one was open for 0% -> 2% of each run, Pallas kernels for 6% -> 6%
where the time goes in v3:
time: 62.5 us; the launch traced here: 62.2 us
  starting transfers between devices  27 us (43%)
  waiting for transfers between devices  21.1 us (34%)
  Pallas kernels  12.2 us (20%)
  local copies, waits for them, and re-layouts  1.02 us (2%)
  other arithmetic  0.85 us (1%)
    ppermute x26, starting transfers between devices, swap_by(): return lax.ppermute(arr, AXES, perm)  27 us
    ppermute x26, waiting for transfers between devices, swap_by(): return lax.ppermute(arr, AXES, perm)  21.1 us
    pallas_call x1, Pallas kernels, on_device(): pl.pallas_call(functools.partial(half_kernel, offsets, far, far_sends, nq...  8.67 us
    pallas_call x1, Pallas kernels, rest(): pl.pallas_call(functools.partial(rest_kernel, orders, edge), out_shape=ch...  3.56 us
  transfers between devices with their start and end apart: 26, of which 15 were waited for; matrix products, arithmetic and copies ran while one was open for 2% of the time, Pallas kernels for 6%

profile of v3, /device:TPU:0, one launch (start us, length us, event | category | flops | bytes accessed | tf_op | source)
XLA Modules:
  0.0 62.2 jit_solution(1238683607659310853)
XLA Ops:
  0.0 3.9 %collective-permute-start.3 = (bf16[256,256]{1,0:T(8,128)(2,1)}, bf16[256,256]{1,0:T(8,128)(2,1)S(1)}, u32[]{:S(2)}, u32[]{:S(2)}) collective-permute-start(bf16[256,256]{1,0:T(8,128)(2,1)} %bitcast.1), channel_id=1, source_target_pairs={{0,17},{1,16},{2,19},{3,18},{4,21},{5,20},{6,23},{7,22},{8,25},{9,... | collective-permute-start | bytes 393224 | tf_op jit(solution)/shard_map/ppermute | solution.py:21
  3.9 0.5 collective-permute-start.2
  4.4 0.1 collective-permute-start.1
  4.5 3.1 %collective-permute-start = (bf16[256,256]{1,0:T(8,128)(2,1)}, bf16[256,256]{1,0:T(8,128)(2,1)S(1)}, u32[]{:S(2)}, u32[]{:S(2)}) collective-permute-start(bf16[256,256]{1,0:T(8,128)(2,1)} %bitcast.4), channel_id=1, source_target_pairs={{0,4},{1,5},{2,6},{3,7},{4,0},{5,1},{6,2},{7,3},{8,12},{9,13},{10,... | collective-permute-start | bytes 393224 | tf_op jit(solution)/shard_map/ppermute | solution.py:21
  7.5 1.0 %concatenate.12 = bf16[512,256]{1,0:T(8,128)(2,1)S(1)} pad(bf16[256,256]{1,0:T(8,128)(2,1)} %bitcast.5, bf16[]{:T(256)} %constant.0.clone.1), padding=0_256x0_0 | pad | bytes 393218 | tf_op jit(solution)/shard_map/concatenate | solution.py:40
  8.5 1.9 %collective-permute-done.2 = bf16[256,256]{1,0:T(8,128)(2,1)S(1)} collective-permute-done((bf16[256,256]{1,0:T(8,128)(2,1)}, bf16[256,256]{1,0:T(8,128)(2,1)S(1)}, u32[]{:S(2)}, u32[]{:S(2)}) %collective-permute-start.2) | collective-permute-done | bytes 131104 | tf_op jit(solution)/shard_map/ppermute | solution.py:21
  10.4 0.3 collective-permute-done.1
  10.7 2.6 %collective-permute-done = bf16[256,256]{1,0:T(8,128)(2,1)S(1)} collective-permute-done((bf16[256,256]{1,0:T(8,128)(2,1)}, bf16[256,256]{1,0:T(8,128)(2,1)S(1)}, u32[]{:S(2)}, u32[]{:S(2)}) %collective-permute-start) | collective-permute-done | bytes 131104 | tf_op jit(solution)/shard_map/ppermute | solution.py:21
  13.2 0.9 %collective-permute-start.4 = (bf16[512,256]{1,0:T(8,128)(2,1)S(1)}, bf16[512,256]{1,0:T(8,128)(2,1)S(1)}, u32[]{:S(2)}, u32[]{:S(2)}) collective-permute-start(bf16[512,256]{1,0:T(8,128)(2,1)S(1)} %constant_dynamic-update-slice_fusion.6.refs_0_), channel_id=1, source_target_pairs={{0,2},{1,3},{2,0},{3,1},{4,6},{5,7},{6,4},{7,5},{8,10},{9,11},{10,... | collective-permute-start | bytes 786440 | tf_op jit(solution)/shard_map/ppermute | solution.py:21
  14.1 2.4 %collective-permute-start.7 = (bf16[256,256]{1,0:T(8,128)(2,1)S(1)}, bf16[256,256]{1,0:T(8,128)(2,1)S(1)}, u32[]{:S(2)}, u32[]{:S(2)}) collective-permute-start(bf16[256,256]{1,0:T(8,128)(2,1)S(1)} %collective-permute-done), channel_id=1, source_target_pairs={{0,17},{1,16},{2,19},{3,18},{4,21},{5,20},{6,23},{7,22},{8,25},{9,... | collective-permute-start | bytes 393224 | tf_op jit(solution)/shard_map/ppermute | solution.py:21
  16.6 0.5 collective-permute-start.6
  17.1 0.5 collective-permute-start.5
  17.6 0.0 collective-permute-start.11
  17.6 3.2 %collective-permute-done.7 = bf16[256,256]{1,0:T(8,128)(2,1)S(1)} collective-permute-done((bf16[256,256]{1,0:T(8,128)(2,1)S(1)}, bf16[256,256]{1,0:T(8,128)(2,1)S(1)}, u32[]{:S(2)}, u32[]{:S(2)}) %collective-permute-start.7) | collective-permute-done | bytes 131104 | tf_op jit(solution)/shard_map/ppermute | solution.py:21
  20.9 1.5 %collective-permute-done.6 = bf16[256,256]{1,0:T(8,128)(2,1)S(1)} collective-permute-done((bf16[256,256]{1,0:T(8,128)(2,1)S(1)}, bf16[256,256]{1,0:T(8,128)(2,1)S(1)}, u32[]{:S(2)}, u32[]{:S(2)}) %collective-permute-start.6) | collective-permute-done | bytes 131104 | tf_op jit(solution)/shard_map/ppermute | solution.py:21
  22.3 0.1 collective-permute-done.5
  22.4 0.0 collective-permute-done.4.refs_4_
  22.4 1.1 %collective-permute-start.10 = (bf16[512,256]{1,0:T(8,128)(2,1)S(1)}, bf16[512,256]{1,0:T(8,128)(2,1)S(1)}, u32[]{:S(2)}, u32[]{:S(2)}) collective-permute-start(bf16[512,256]{1,0:T(8,128)(2,1)S(1)} %constant_dynamic-update-slice_fusion.4.refs_3_), channel_id=1, source_target_pairs={{0,2},{1,3},{2,0},{3,1},{4,6},{5,7},{6,4},{7,5},{8,10},{9,11},{10,... | collective-permute-start | bytes 786440 | tf_op jit(solution)/shard_map/ppermute | solution.py:21
  23.5 1.5 %collective-permute-start.9 = (bf16[512,256]{1,0:T(8,128)(2,1)S(1)}, bf16[512,256]{1,0:T(8,128)(2,1)S(1)}, u32[]{:S(2)}, u32[]{:S(2)}) collective-permute-start(bf16[512,256]{1,0:T(8,128)(2,1)S(1)} %collective-permute-done.4.refs_4_), channel_id=1, source_target_pairs={{0,1},{1,0},{2,3},{3,2},{4,5},{5,4},{6,7},{7,6},{8,9},{9,8},{10,11... | collective-permute-start | bytes 786440 | tf_op jit(solution)/shard_map/ppermute | solution.py:21
  25.0 0.5 collective-permute-start.8
  25.5 0.1 collective-permute-start.13
  25.6 4.0 %collective-permute-done.10.refs_7_ = bf16[512,256]{1,0:T(8,128)(2,1)S(1)} collective-permute-done((bf16[512,256]{1,0:T(8,128)(2,1)S(1)}, bf16[512,256]{1,0:T(8,128)(2,1)S(1)}, u32[]{:S(2)}, u32[]{:S(2)}) %collective-permute-start.10) | collective-permute-done | bytes 262176 | tf_op jit(solution)/shard_map/ppermute | solution.py:21
  29.7 0.0 collective-permute-start.12
  29.7 0.3 collective-permute-done.9.refs_6_
  29.9 0.3 collective-permute-start.14
  30.2 1.2 %collective-permute-done.8.refs_5_ = bf16[512,256]{1,0:T(8,128)(2,1)S(1)} collective-permute-done((bf16[512,256]{1,0:T(8,128)(2,1)S(1)}, bf16[512,256]{1,0:T(8,128)(2,1)S(1)}, u32[]{:S(2)}, u32[]{:S(2)}) %collective-permute-start.8) | collective-permute-done | bytes 262176 | tf_op jit(solution)/shard_map/ppermute | solution.py:21
  31.4 0.5 collective-permute-start.16
  31.9 0.1 collective-permute-start.17
  31.9 0.0 collective-permute-done.12.refs_9_
  31.9 0.4 collective-permute-start.18
  32.4 0.5 collective-permute-done.15.refs_12_
  32.9 0.4 collective-permute-done.16.refs_13_
  33.3 0.4 collective-permute-done.17.refs_14_
  33.6 0.4 collective-permute-done.18.refs_15_
  34.0 8.7 %shard_map.55 = (bf16[1,512,128]{2,1,0:T(8,128)(2,1)S(1)}, bf16[1,512,128]{2,1,0:T(8,128)(2,1)S(1)}, bf16[1,512,128]{2,1,0:T(8,128)(2,1)S(1)}, bf16[16,64,1536]{...) custom-call(s32[3,4]{1,0:T(4,128)} %match_hbm.1, s32[3,1,1,2,48]{4,3,2,1,0:T(2,128)} %lists_hbm.1, s32[1,2,64]{2,1,0:T(2,128)} %ex_hbm.3, ...), custom_call_target="tpu_custom_call" | custom-call | tf_op jit(solution)/shard_map/pallas_call | solution.py:215
  42.7 0.9 %collective-permute-start.19 = (bf16[1,512,128]{2,1,0:T(8,128)(2,1)S(1)}, bf16[1,512,128]{2,1,0:T(8,128)(2,1)S(1)}, u32[]{:S(2)}, u32[]{:S(2)}) collective-permute-start(bf16[1,512,128]{2,1,0:T(8,128)(2,1)S(1)} %get-tuple-element.41), channel_id=1, source_target_pairs={{0,1},{1,0},{2,3},{3,2},{4,5},{5,4},{6,7},{7,6},{8,9},{9,8},{10,11... | collective-permute-start | bytes 393224 | tf_op jit(solution)/shard_map/ppermute | solution.py:21
  43.6 1.4 %collective-permute-start.20 = (bf16[1,512,128]{2,1,0:T(8,128)(2,1)S(1)}, bf16[1,512,128]{2,1,0:T(8,128)(2,1)S(1)}, u32[]{:S(2)}, u32[]{:S(2)}) collective-permute-start(bf16[1,512,128]{2,1,0:T(8,128)(2,1)S(1)} %get-tuple-element.42), channel_id=1, source_target_pairs={{0,2},{1,3},{2,0},{3,1},{4,6},{5,7},{6,4},{7,5},{8,10},{9,11},{10,... | collective-permute-start | bytes 393224 | tf_op jit(solution)/shard_map/ppermute | solution.py:21
  45.1 1.2 %collective-permute-start.21 = (bf16[1,512,128]{2,1,0:T(8,128)(2,1)S(1)}, bf16[1,512,128]{2,1,0:T(8,128)(2,1)S(1)}, u32[]{:S(2)}, u32[]{:S(2)}) collective-permute-start(bf16[1,512,128]{2,1,0:T(8,128)(2,1)S(1)} %get-tuple-element.43), channel_id=1, source_target_pairs={{0,3},{1,2},{2,1},{3,0},{4,7},{5,6},{6,5},{7,4},{8,11},{9,10},{10,... | collective-permute-start | bytes 393224 | tf_op jit(solution)/shard_map/ppermute | solution.py:21
  46.2 3.6 %shard_map.56 = (bf16[1,512,128]{2,1,0:T(8,128)(2,1)S(1)}, bf16[1,512,128]{2,1,0:T(8,128)(2,1)S(1)}, bf16[1,512,128]{2,1,0:T(8,128)(2,1)S(1)}, f32[2,512,128]{2,1,0:T(8,128)S(1)}) custom-call(s32[1,2,64]{2,1,0:T(2,128)} %ex_hbm.3, bf16[16,64,1536]{2,1,0:T(8,128)(2,1)S(1)} %get-tuple-element.38.x_ref, bf16[16,1536,128]{2,1,0:T(8,128)(2,1)S(1)} %get-tuple-element.39.turned_ref), custom_call_target="tpu_custom_call" | custom-call | flops 805306368 | bytes 8388608 | tf_op jit(solution)/shard_map/pallas_call | solution.py:240
  49.8 0.9 %collective-permute-start.23 = (bf16[1,512,128]{2,1,0:T(8,128)(2,1)S(1)}, bf16[1,512,128]{2,1,0:T(8,128)(2,1)S(1)}, u32[]{:S(2)}, u32[]{:S(2)}) collective-permute-start(bf16[1,512,128]{2,1,0:T(8,128)(2,1)S(1)} %get-tuple-element.44), channel_id=1, source_target_pairs={{0,1},{1,0},{2,3},{3,2},{4,5},{5,4},{6,7},{7,6},{8,9},{9,8},{10,11... | collective-permute-start | bytes 393224 | tf_op jit(solution)/shard_map/ppermute | solution.py:21
  50.8 1.4 %collective-permute-start.24 = (bf16[1,512,128]{2,1,0:T(8,128)(2,1)S(1)}, bf16[1,512,128]{2,1,0:T(8,128)(2,1)S(1)}, u32[]{:S(2)}, u32[]{:S(2)}) collective-permute-start(bf16[1,512,128]{2,1,0:T(8,128)(2,1)S(1)} %get-tuple-element.45), channel_id=1, source_target_pairs={{0,2},{1,3},{2,0},{3,1},{4,6},{5,7},{6,4},{7,5},{8,10},{9,11},{10,... | collective-permute-start | bytes 393224 | tf_op jit(solution)/shard_map/ppermute | solution.py:21
  52.2 1.2 %collective-permute-start.25 = (bf16[1,512,128]{2,1,0:T(8,128)(2,1)S(1)}, bf16[1,512,128]{2,1,0:T(8,128)(2,1)S(1)}, u32[]{:S(2)}, u32[]{:S(2)}) collective-permute-start(bf16[1,512,128]{2,1,0:T(8,128)(2,1)S(1)} %get-tuple-element.46), channel_id=1, source_target_pairs={{0,3},{1,2},{2,1},{3,0},{4,7},{5,6},{6,5},{7,4},{8,11},{9,10},{10,... | collective-permute-start | bytes 393224 | tf_op jit(solution)/shard_map/ppermute | solution.py:21
  53.4 0.0 collective-permute-done.21
  53.4 0.1 add_convert_fusion
  53.4 3.6 %collective-permute-start.22 = (bf16[1,512,128]{2,1,0:T(8,128)(2,1)S(1)}, bf16[1,512,128]{2,1,0:T(8,128)(2,1)S(1)}, u32[]{:S(2)}, u32[]{:S(2)}) collective-permute-start(bf16[1,512,128]{2,1,0:T(8,128)(2,1)S(1)} %add_convert_fusion), channel_id=1, source_target_pairs={{0,4},{1,5},{2,6},{3,7},{4,0},{5,1},{6,2},{7,3},{8,12},{9,13},{10,... | collective-permute-start | bytes 393224 | tf_op jit(solution)/shard_map/ppermute | solution.py:21
  57.0 1.5 %collective-permute-done.24 = bf16[1,512,128]{2,1,0:T(8,128)(2,1)S(1)} collective-permute-done((bf16[1,512,128]{2,1,0:T(8,128)(2,1)S(1)}, bf16[1,512,128]{2,1,0:T(8,128)(2,1)S(1)}, u32[]{:S(2)}, u32[]{:S(2)}) %collective-permute-start.24) | collective-permute-done | bytes 131104 | tf_op jit(solution)/shard_map/ppermute | solution.py:21
  58.5 2.9 %collective-permute-done.25 = bf16[1,512,128]{2,1,0:T(8,128)(2,1)S(1)} collective-permute-done((bf16[1,512,128]{2,1,0:T(8,128)(2,1)S(1)}, bf16[1,512,128]{2,1,0:T(8,128)(2,1)S(1)}, u32[]{:S(2)}, u32[]{:S(2)}) %collective-permute-start.25) | collective-permute-done | bytes 131104 | tf_op jit(solution)/shard_map/ppermute | solution.py:21
  61.5 0.8 %add_multiply_fusion = f32[1,512,128]{2,1,0:T(8,128)} fusion(bf16[1,512,128]{2,1,0:T(8,128)(2,1)S(1)} %collective-permute-done.25, bf16[1,512,128]{2,1,0:T(8,128)(2,1)S(1)} %collective-permute-done.24, bf16[1,512,128]{2,1,0:T(8,128)(2,1)S(1)} %collective-permute-done.23, bf16[1,512,128]{2,1,0:T(8,128)(2,1)S(1)} %collective-permute-done.22, ...), kind=kLoop, calls=%fused_computation | loop fusion | flops 589824 | bytes 1048576 | tf_op jit(solution)/shard_map/mul | solution.py:269
  (16 shorter events, 0.1 us)
Async XLA Ops:
  0.0 8.5 %collective-permute-start.3 = (bf16[256,256]{1,0:T(8,128)(2,1)}, bf16[256,256]{1,0:T(8,128)(2,1)S(1)}, u32[]{:S(2)}, u32[]{:S(2)}) collective-permute-start(bf16[256,256]{1,0:T(8,128)(2,1)} %bitcast.1), channel_id=1, source_target_pairs={{0,17},{1,16},{2,19},{3,18},{4,21},{5,20},{6,23},{7,22},{8,25},{9,... | collective-permute-start | bytes 393224 | tf_op jit(solution)/shard_map/ppermute | solution.py:21
  3.9 6.5 %collective-permute-start.2 = (bf16[256,256]{1,0:T(8,128)(2,1)}, bf16[256,256]{1,0:T(8,128)(2,1)S(1)}, u32[]{:S(2)}, u32[]{:S(2)}) collective-permute-start(bf16[256,256]{1,0:T(8,128)(2,1)} %bitcast.2), channel_id=1, source_target_pairs={{0,1},{1,0},{2,3},{3,2},{4,5},{5,4},{6,7},{7,6},{8,9},{9,8},{10,11... | collective-permute-start | bytes 393224 | tf_op jit(solution)/shard_map/ppermute | solution.py:21
  4.4 6.3 %collective-permute-start.1 = (bf16[256,256]{1,0:T(8,128)(2,1)}, bf16[256,256]{1,0:T(8,128)(2,1)S(1)}, u32[]{:S(2)}, u32[]{:S(2)}) collective-permute-start(bf16[256,256]{1,0:T(8,128)(2,1)} %bitcast.3), channel_id=1, source_target_pairs={{0,16},{1,17},{2,18},{3,19},{4,20},{5,21},{6,22},{7,23},{8,24},{9,... | collective-permute-start | bytes 393224 | tf_op jit(solution)/shard_map/ppermute | solution.py:21
  4.5 8.8 %collective-permute-start = (bf16[256,256]{1,0:T(8,128)(2,1)}, bf16[256,256]{1,0:T(8,128)(2,1)S(1)}, u32[]{:S(2)}, u32[]{:S(2)}) collective-permute-start(bf16[256,256]{1,0:T(8,128)(2,1)} %bitcast.4), channel_id=1, source_target_pairs={{0,4},{1,5},{2,6},{3,7},{4,0},{5,1},{6,2},{7,3},{8,12},{9,13},{10,... | collective-permute-start | bytes 393224 | tf_op jit(solution)/shard_map/ppermute | solution.py:21
  13.2 9.2 %collective-permute-start.4 = (bf16[512,256]{1,0:T(8,128)(2,1)S(1)}, bf16[512,256]{1,0:T(8,128)(2,1)S(1)}, u32[]{:S(2)}, u32[]{:S(2)}) collective-permute-start(bf16[512,256]{1,0:T(8,128)(2,1)S(1)} %constant_dynamic-update-slice_fusion.6.refs_0_), channel_id=1, source_target_pairs={{0,2},{1,3},{2,0},{3,1},{4,6},{5,7},{6,4},{7,5},{8,10},{9,11},{10,... | collective-permute-start | bytes 786440 | tf_op jit(solution)/shard_map/ppermute | solution.py:21
  14.1 6.8 %collective-permute-start.7 = (bf16[256,256]{1,0:T(8,128)(2,1)S(1)}, bf16[256,256]{1,0:T(8,128)(2,1)S(1)}, u32[]{:S(2)}, u32[]{:S(2)}) collective-permute-start(bf16[256,256]{1,0:T(8,128)(2,1)S(1)} %collective-permute-done), channel_id=1, source_target_pairs={{0,17},{1,16},{2,19},{3,18},{4,21},{5,20},{6,23},{7,22},{8,25},{9,... | collective-permute-start | bytes 393224 | tf_op jit(solution)/shard_map/ppermute | solution.py:21
  16.6 5.8 %collective-permute-start.6 = (bf16[256,256]{1,0:T(8,128)(2,1)S(1)}, bf16[256,256]{1,0:T(8,128)(2,1)S(1)}, u32[]{:S(2)}, u32[]{:S(2)}) collective-permute-start(bf16[256,256]{1,0:T(8,128)(2,1)S(1)} %collective-permute-done), channel_id=1, source_target_pairs={{0,1},{1,0},{2,3},{3,2},{4,5},{5,4},{6,7},{7,6},{8,9},{9,8},{10,11... | collective-permute-start | bytes 393224 | tf_op jit(solution)/shard_map/ppermute | solution.py:21
  17.1 5.3 %collective-permute-start.5 = (bf16[256,256]{1,0:T(8,128)(2,1)S(1)}, bf16[256,256]{1,0:T(8,128)(2,1)S(1)}, u32[]{:S(2)}, u32[]{:S(2)}) collective-permute-start(bf16[256,256]{1,0:T(8,128)(2,1)S(1)} %collective-permute-done), channel_id=1, source_target_pairs={{0,16},{1,17},{2,18},{3,19},{4,20},{5,21},{6,22},{7,23},{8,24},{9,... | collective-permute-start | bytes 393224 | tf_op jit(solution)/shard_map/ppermute | solution.py:21
  17.6 13.8 %collective-permute-start.11 = (bf16[512,256]{1,0:T(8,128)(2,1)S(1)}, bf16[512,256]{1,0:T(8,128)(2,1)S(1)}, u32[]{:S(2)}, u32[]{:S(2)}) collective-permute-start(bf16[512,256]{1,0:T(8,128)(2,1)S(1)} %constant_dynamic-update-slice_fusion.6.refs_0_), channel_id=1, source_target_pairs={{0,8},{1,9},{2,10},{3,11},{4,12},{5,13},{6,14},{7,15},{8,0},{9,1},... | collective-permute-start | bytes 786440 | tf_op jit(solution)/shard_map/ppermute | solution.py:21
  22.4 7.3 %collective-permute-start.10 = (bf16[512,256]{1,0:T(8,128)(2,1)S(1)}, bf16[512,256]{1,0:T(8,128)(2,1)S(1)}, u32[]{:S(2)}, u32[]{:S(2)}) collective-permute-start(bf16[512,256]{1,0:T(8,128)(2,1)S(1)} %constant_dynamic-update-slice_fusion.4.refs_3_), channel_id=1, source_target_pairs={{0,2},{1,3},{2,0},{3,1},{4,6},{5,7},{6,4},{7,5},{8,10},{9,11},{10,... | collective-permute-start | bytes 786440 | tf_op jit(solution)/shard_map/ppermute | solution.py:21
  23.5 6.4 %collective-permute-start.9 = (bf16[512,256]{1,0:T(8,128)(2,1)S(1)}, bf16[512,256]{1,0:T(8,128)(2,1)S(1)}, u32[]{:S(2)}, u32[]{:S(2)}) collective-permute-start(bf16[512,256]{1,0:T(8,128)(2,1)S(1)} %collective-permute-done.4.refs_4_), channel_id=1, source_target_pairs={{0,1},{1,0},{2,3},{3,2},{4,5},{5,4},{6,7},{7,6},{8,9},{9,8},{10,11... | collective-permute-start | bytes 786440 | tf_op jit(solution)/shard_map/ppermute | solution.py:21
  25.0 6.4 %collective-permute-start.8 = (bf16[512,256]{1,0:T(8,128)(2,1)S(1)}, bf16[512,256]{1,0:T(8,128)(2,1)S(1)}, u32[]{:S(2)}, u32[]{:S(2)}) collective-permute-start(bf16[512,256]{1,0:T(8,128)(2,1)S(1)} %collective-permute-done.4.refs_4_), channel_id=1, source_target_pairs={{0,16},{1,17},{2,18},{3,19},{4,20},{5,21},{6,22},{7,23},{8,24},{9,... | collective-permute-start | bytes 786440 | tf_op jit(solution)/shard_map/ppermute | solution.py:21
  25.5 6.3 %collective-permute-start.13 = (bf16[512,256]{1,0:T(8,128)(2,1)S(1)}, bf16[512,256]{1,0:T(8,128)(2,1)S(1)}, u32[]{:S(2)}, u32[]{:S(2)}) collective-permute-start(bf16[512,256]{1,0:T(8,128)(2,1)S(1)} %constant_dynamic-update-slice_fusion.2.refs_2_), channel_id=1, source_target_pairs={{0,8},{1,9},{2,10},{3,11},{4,12},{5,13},{6,14},{7,15},{8,0},{9,1},... | collective-permute-start | bytes 786440 | tf_op jit(solution)/shard_map/ppermute | solution.py:21
  29.7 2.3 %collective-permute-start.12 = (bf16[512,256]{1,0:T(8,128)(2,1)S(1)}, bf16[512,256]{1,0:T(8,128)(2,1)S(1)}, u32[]{:S(2)}, u32[]{:S(2)}) collective-permute-start(bf16[512,256]{1,0:T(8,128)(2,1)S(1)} %constant_dynamic-update-slice_fusion.refs_1_), channel_id=1, source_target_pairs={{0,8},{1,9},{2,10},{3,11},{4,12},{5,13},{6,14},{7,15},{8,0},{9,1},... | collective-permute-start | bytes 786440 | tf_op jit(solution)/shard_map/ppermute | solution.py:21
  29.9 2.4 %collective-permute-start.14 = (bf16[512,256]{1,0:T(8,128)(2,1)S(1)}, bf16[512,256]{1,0:T(8,128)(2,1)S(1)}, u32[]{:S(2)}, u32[]{:S(2)}) collective-permute-start(bf16[512,256]{1,0:T(8,128)(2,1)S(1)} %constant_dynamic-update-slice_fusion.4.refs_3_), channel_id=1, source_target_pairs={{0,8},{1,9},{2,10},{3,11},{4,12},{5,13},{6,14},{7,15},{8,0},{9,1},... | collective-permute-start | bytes 786440 | tf_op jit(solution)/shard_map/ppermute | solution.py:21
  31.4 1.5 %collective-permute-start.15 = (bf16[512,256]{1,0:T(8,128)(2,1)S(1)}, bf16[512,256]{1,0:T(8,128)(2,1)S(1)}, u32[]{:S(2)}, u32[]{:S(2)}) collective-permute-start(bf16[512,256]{1,0:T(8,128)(2,1)S(1)} %collective-permute-done.4.refs_4_), channel_id=1, source_target_pairs={{0,8},{1,9},{2,10},{3,11},{4,12},{5,13},{6,14},{7,15},{8,0},{9,1},... | collective-permute-start | bytes 786440 | tf_op jit(solution)/shard_map/ppermute | solution.py:21
  31.4 1.9 %collective-permute-start.16 = (bf16[512,256]{1,0:T(8,128)(2,1)S(1)}, bf16[512,256]{1,0:T(8,128)(2,1)S(1)}, u32[]{:S(2)}, u32[]{:S(2)}) collective-permute-start(bf16[512,256]{1,0:T(8,128)(2,1)S(1)} %collective-permute-done.8.refs_5_), channel_id=1, source_target_pairs={{0,8},{1,9},{2,10},{3,11},{4,12},{5,13},{6,14},{7,15},{8,0},{9,1},... | collective-permute-start | bytes 786440 | tf_op jit(solution)/shard_map/ppermute | solution.py:21
  31.9 1.8 %collective-permute-start.17 = (bf16[512,256]{1,0:T(8,128)(2,1)S(1)}, bf16[512,256]{1,0:T(8,128)(2,1)S(1)}, u32[]{:S(2)}, u32[]{:S(2)}) collective-permute-start(bf16[512,256]{1,0:T(8,128)(2,1)S(1)} %collective-permute-done.9.refs_6_), channel_id=1, source_target_pairs={{0,8},{1,9},{2,10},{3,11},{4,12},{5,13},{6,14},{7,15},{8,0},{9,1},... | collective-permute-start | bytes 786440 | tf_op jit(solution)/shard_map/ppermute | solution.py:21
  31.9 2.1 %collective-permute-start.18 = (bf16[512,256]{1,0:T(8,128)(2,1)S(1)}, bf16[512,256]{1,0:T(8,128)(2,1)S(1)}, u32[]{:S(2)}, u32[]{:S(2)}) collective-permute-start(bf16[512,256]{1,0:T(8,128)(2,1)S(1)} %collective-permute-done.10.refs_7_), channel_id=1, source_target_pairs={{0,8},{1,9},{2,10},{3,11},{4,12},{5,13},{6,14},{7,15},{8,0},{9,1},... | collective-permute-start | bytes 786440 | tf_op jit(solution)/shard_map/ppermute | solution.py:21
  42.7 9.5 %collective-permute-start.19 = (bf16[1,512,128]{2,1,0:T(8,128)(2,1)S(1)}, bf16[1,512,128]{2,1,0:T(8,128)(2,1)S(1)}, u32[]{:S(2)}, u32[]{:S(2)}) collective-permute-start(bf16[1,512,128]{2,1,0:T(8,128)(2,1)S(1)} %get-tuple-element.41), channel_id=1, source_target_pairs={{0,1},{1,0},{2,3},{3,2},{4,5},{5,4},{6,7},{7,6},{8,9},{9,8},{10,11... | collective-permute-start | bytes 393224 | tf_op jit(solution)/shard_map/ppermute | solution.py:21
  43.6 9.7 %collective-permute-start.20 = (bf16[1,512,128]{2,1,0:T(8,128)(2,1)S(1)}, bf16[1,512,128]{2,1,0:T(8,128)(2,1)S(1)}, u32[]{:S(2)}, u32[]{:S(2)}) collective-permute-start(bf16[1,512,128]{2,1,0:T(8,128)(2,1)S(1)} %get-tuple-element.42), channel_id=1, source_target_pairs={{0,2},{1,3},{2,0},{3,1},{4,6},{5,7},{6,4},{7,5},{8,10},{9,11},{10,... | collective-permute-start | bytes 393224 | tf_op jit(solution)/shard_map/ppermute | solution.py:21
  45.1 8.3 %collective-permute-start.21 = (bf16[1,512,128]{2,1,0:T(8,128)(2,1)S(1)}, bf16[1,512,128]{2,1,0:T(8,128)(2,1)S(1)}, u32[]{:S(2)}, u32[]{:S(2)}) collective-permute-start(bf16[1,512,128]{2,1,0:T(8,128)(2,1)S(1)} %get-tuple-element.43), channel_id=1, source_target_pairs={{0,3},{1,2},{2,1},{3,0},{4,7},{5,6},{6,5},{7,4},{8,11},{9,10},{10,... | collective-permute-start | bytes 393224 | tf_op jit(solution)/shard_map/ppermute | solution.py:21
  49.8 7.2 %collective-permute-start.23 = (bf16[1,512,128]{2,1,0:T(8,128)(2,1)S(1)}, bf16[1,512,128]{2,1,0:T(8,128)(2,1)S(1)}, u32[]{:S(2)}, u32[]{:S(2)}) collective-permute-start(bf16[1,512,128]{2,1,0:T(8,128)(2,1)S(1)} %get-tuple-element.44), channel_id=1, source_target_pairs={{0,1},{1,0},{2,3},{3,2},{4,5},{5,4},{6,7},{7,6},{8,9},{9,8},{10,11... | collective-permute-start | bytes 393224 | tf_op jit(solution)/shard_map/ppermute | solution.py:21
  50.8 7.7 %collective-permute-start.24 = (bf16[1,512,128]{2,1,0:T(8,128)(2,1)S(1)}, bf16[1,512,128]{2,1,0:T(8,128)(2,1)S(1)}, u32[]{:S(2)}, u32[]{:S(2)}) collective-permute-start(bf16[1,512,128]{2,1,0:T(8,128)(2,1)S(1)} %get-tuple-element.45), channel_id=1, source_target_pairs={{0,2},{1,3},{2,0},{3,1},{4,6},{5,7},{6,4},{7,5},{8,10},{9,11},{10,... | collective-permute-start | bytes 393224 | tf_op jit(solution)/shard_map/ppermute | solution.py:21
  52.2 9.3 %collective-permute-start.25 = (bf16[1,512,128]{2,1,0:T(8,128)(2,1)S(1)}, bf16[1,512,128]{2,1,0:T(8,128)(2,1)S(1)}, u32[]{:S(2)}, u32[]{:S(2)}) collective-permute-start(bf16[1,512,128]{2,1,0:T(8,128)(2,1)S(1)} %get-tuple-element.46), channel_id=1, source_target_pairs={{0,3},{1,2},{2,1},{3,0},{4,7},{5,6},{6,5},{7,4},{8,11},{9,10},{10,... | collective-permute-start | bytes 393224 | tf_op jit(solution)/shard_map/ppermute | solution.py:21
  53.4 8.0 %collective-permute-start.22 = (bf16[1,512,128]{2,1,0:T(8,128)(2,1)S(1)}, bf16[1,512,128]{2,1,0:T(8,128)(2,1)S(1)}, u32[]{:S(2)}, u32[]{:S(2)}) collective-permute-start(bf16[1,512,128]{2,1,0:T(8,128)(2,1)S(1)} %add_convert_fusion), channel_id=1, source_target_pairs={{0,4},{1,5},{2,6},{3,7},{4,0},{5,1},{6,2},{7,3},{8,12},{9,13},{10,... | collective-permute-start | bytes 393224 | tf_op jit(solution)/shard_map/ppermute | solution.py:21
